TPU v7x, 32 devices: a whole 2x2x4 slice. The times are simulated.
32 devices in a mesh: row: 4 (over y, x), col: 8 (over z, core).
Axes of the slice: x: 2, y: 2, z: 4, core: 2. Of those that a mesh axis runs over, the one named last changes fastest.
Arguments:
- matrix: float32 [8, 1024, 4, 2048], P(None, 'row', None, 'col'), may hold values from -8 to 8, as said below
Outputs:
- reduced: float32 [8, 1024, 4, 2048], P(None, 'row', None, 'col')
Inputs may be any that keep to these rules, and one draw needn't show every extreme that they name: symmetric: the entries at (r, c) and (c, r) of the 8192 x 8192 matrix are equal.
All inputs are finite; a program needn't handle non-finite values.
Results may differ from a plain program's by a relative error of at most 0.0002.
Values sent between devices are 32-bit elements; how exact they have to be, the bound alone decides.
A program may use at most 128 MiB of HBM per device.

v0:
```python
import jax
import jax.numpy as jnp
from jax import lax
from jax.sharding import PartitionSpec as P

PANELS = 2


highest = lax.Precision.HIGHEST


def broadcast(value, axis, root):
    mine = lax.axis_index(axis) == root
    return lax.psum(jnp.where(mine, value, jnp.zeros_like(value)), axis)


def matmul(left, right):
    return jnp.dot(left, right, precision=highest, preferred_element_type=jnp.float32)


def identity_rows(global_index, start, width):
    offsets = global_index[:, None] - start
    return (offsets == jnp.arange(width, dtype=jnp.int32)[None, :]).astype(jnp.float32)


def shards(matrix):
    row_blocks, width, col_blocks, _ = matrix.shape
    row_devices = lax.axis_size("row")
    col_devices = lax.axis_size("col")
    row_index = lax.axis_index("row")
    col_index = lax.axis_index("col")
    local_rows = row_blocks * width
    local_cols = col_blocks * width
    dense = matrix.reshape(local_rows, local_cols)
    row_range = jnp.arange(local_rows, dtype=jnp.int32)
    col_range = jnp.arange(local_cols, dtype=jnp.int32)
    global_rows = (row_range // width * row_devices + row_index) * width + row_range % width
    global_cols = (col_range // width * col_devices + col_index) * width + col_range % width
    extract_col_slot = 0 // col_devices * width
    extract_row_slot = 0 // row_devices * width
    col_panel = dense[:, extract_col_slot : extract_col_slot + width]
    row_panel = dense[extract_row_slot : extract_row_slot + width, :]
    for panel in range(PANELS):
        start = (panel + 1) * width
        low_rows = jnp.where(global_rows[:, None] >= start, col_panel, 0.0)
        low_rows = broadcast(low_rows, "col", panel % col_devices)
        right_cols = jnp.where(global_cols[None, :] >= start, row_panel, 0.0)
        right_cols = broadcast(right_cols, "row", panel % row_devices)
        top_slot = (panel + 1) // row_devices * width
        top_part = jnp.where(
            row_index == (panel + 1) % row_devices, low_rows[top_slot : top_slot + width], 0.0
        )
        gram_sum, top_block = lax.psum((matmul(low_rows.T, low_rows), top_part), "row")
        factor = jnp.linalg.cholesky(gram_sum)
        basis_rows = jax.scipy.linalg.solve_triangular(factor, low_rows.T, lower=True).T
        basis_cols = jax.scipy.linalg.solve_triangular(factor, right_cols, lower=True).T
        basis_top = jax.scipy.linalg.solve_triangular(factor, top_block.T, lower=True).T
        shifted = jnp.eye(width, dtype=jnp.float32) + basis_top
        normal = matmul(shifted.T, shifted)
        coupling = jax.scipy.linalg.cho_solve((jnp.linalg.cholesky(normal), True), shifted.T)
        placed_rows = identity_rows(global_rows, start, width)
        placed_cols = identity_rows(global_cols, start, width)
        vec_rows = basis_rows + placed_rows
        vec_cols = basis_cols + placed_cols
        applied_rows = lax.psum(matmul(dense, vec_cols), "col")
        applied_rows = jnp.where(global_rows[:, None] >= start, applied_rows, 0.0)
        inner = lax.psum(matmul(vec_rows.T, applied_rows), "row")
        middle = matmul(matmul(coupling, inner), coupling.T)
        factor_rows = matmul(applied_rows, coupling.T) - 0.5 * matmul(vec_rows, middle)
        applied_cols = lax.psum(matmul(dense.T, vec_rows), "row")
        applied_cols = jnp.where(global_cols[:, None] >= start, applied_cols, 0.0)
        factor_cols = matmul(applied_cols, coupling.T) - 0.5 * matmul(vec_cols, middle)
        before = dense
        dense = dense - matmul(factor_rows, vec_cols.T) - matmul(vec_rows, factor_cols.T)
        col_slot = panel // col_devices * width
        old_col = dense[:, col_slot : col_slot + width]
        new_col = jnp.where(global_rows[:, None] >= start, matmul(placed_rows, -factor.T), old_col)
        dense = dense.at[:, col_slot : col_slot + width].set(
            jnp.where(col_index == panel % col_devices, new_col, old_col)
        )
        row_slot = panel // row_devices * width
        old_row = dense[row_slot : row_slot + width, :]
        new_row = jnp.where(global_cols[None, :] >= start, matmul(-factor, placed_cols.T), old_row)
        dense = dense.at[row_slot : row_slot + width, :].set(
            jnp.where(row_index == panel % row_devices, new_row, old_row)
        )
        if panel + 1 < PANELS:
            next_col_slot = (panel + 1) // col_devices * width
            next_row_slot = (panel + 1) // row_devices * width
            col_panel = (
                before[:, next_col_slot : next_col_slot + width]
                - matmul(factor_rows, vec_cols[next_col_slot : next_col_slot + width].T)
                - matmul(vec_rows, factor_cols[next_col_slot : next_col_slot + width].T)
            )
            row_panel = (
                before[next_row_slot : next_row_slot + width, :]
                - matmul(factor_rows[next_row_slot : next_row_slot + width], vec_cols.T)
                - matmul(vec_rows[next_row_slot : next_row_slot + width], factor_cols.T)
            )
    return dense.reshape(matrix.shape)


def solution(mesh):
    in_specs = (P(None, "row", None, "col"),)
    out_specs = P(None, "row", None, "col")
    return jax.shard_map(shards, mesh=mesh, in_specs=in_specs, out_specs=out_specs, check_vma=False)
```

profile of v0, /device:TPU:0, one launch (start us, length us, event | category | flops | bytes accessed | tf_op | source)
XLA Modules:
  0.0 930.4 jit_solution(10798614724223404654)
XLA Ops:
  6.5 8.9 copy.40
  15.4 9.2 copy.39
  24.7 3.3 select_select_fusion.2
  28.0 1.4 slice.178
  31.2 64.5 %all-reduce.14.cloned.1.call-done = f32[2048,256]{0,1:T(8,128)} async-done(((f32[2048,256]{0,1:T(8,128)}), f32[2048,256]{0,1:T(8,128)}) %all-reduce.14.cloned.1.call-update) | async-done | bytes 2097168 | tf_op jit(solution)/shard_map/psum | solution.py:14
  95.7 4.9 fusion.201
  102.2 54.9 %all-reduce.28.cloned.1.call-done = (f32[256,1024]{0,1:T(8,128)}, f32[256,256]{0,1:T(8,128)}) async-done(((f32[256,1024]{0,1:T(8,128)}, f32[256,256]{0,1:T(8,128)}), (f32[256,1024]{0,1:T(8,128)}, f32[256,256]{0,1:T(8,128)})) %all-reduce.28.cloned.1.call-update) | async-done | bytes 1310736 | tf_op jit(solution)/shard_map/psum | solution.py:14
  160.0 11.7 %cholesky.214 = f32[128,128]{1,0:T(8,128)S(1)} custom-call(f32[128,128]{1,0:T(8,128)S(1)} %cholesky.346), custom_call_target="Cholesky" | custom-call | tf_op jit(solution)/shard_map/jit(cholesky)/cholesky | solution.py:54
  172.3 9.8 %custom-call.31 = f32[1,128,128]{1,2,0:T(8,128)S(1)} custom-call(f32[1,128,128]{2,1,0:T(8,128)S(1)} %get-tuple-element.203), custom_call_target="InvertDiagBlocksLowerTriangular" | custom-call | tf_op jit(solution)/shard_map/jit(cholesky)/cholesky | solution.py:54
  184.2 11.7 %cholesky.231 = f32[128,128]{1,0:T(8,128)S(1)} custom-call(f32[128,128]{1,0:T(8,128)S(1)} %convolution_subtract_fusion.17), custom_call_target="Cholesky" | custom-call | tf_op jit(solution)/shard_map/jit(cholesky)/cholesky | solution.py:54
  200.7 5.4 while.26
  206.8 20.5 %custom-call.32 = f32[2,128,128]{1,2,0:T(8,128)S(1)} custom-call(f32[2,128,128]{2,1,0:T(8,128)} %copy-done.28), custom_call_target="InvertDiagBlocksLowerTriangular" | custom-call | tf_op jit(solution)/shard_map/jit(_solve_triangular)/triangular_solve | solution.py:56
  227.9 2.0 convolution_subtract_fusion.7
  230.8 10.6 %convolution_bitcast_fusion = f32[2048,256]{0,1:T(8,128)} fusion(f32[1024,256]{0,1:T(8,128)S(1)} %fusion.26, f32[2048,1024]{1,0:T(8,128)} %bitcast.267), kind=kOutput, calls=%fused_computation.22 | convolution fusion | flops 6442450944 | bytes 11534336 | tf_op jit(solution)/shard_map/dot_general | solution.py:18
  244.9 16.7 %convolution_bitcast_fusion.1 = f32[1024,256]{1,0:T(8,128)} fusion(f32[2048,256]{0,1:T(8,128)S(1)} %fusion.6, f32[2048,1024]{1,0:T(8,128)} %bitcast.268), kind=kOutput, calls=%fused_computation.44 | convolution fusion | flops 6442450944 | bytes 11534336 | tf_op jit(solution)/shard_map/dot_general | solution.py:18
  261.6 45.0 %all-reduce.16.cloned.1.call-done = f32[2048,256]{0,1:T(8,128)} async-done(((f32[2048,256]{0,1:T(8,128)}), f32[2048,256]{0,1:T(8,128)}) %all-reduce.16.cloned.1.call-update) | async-done | bytes 2097168 | tf_op jit(solution)/shard_map/psum | solution.py:65
  306.6 4.2 fusion.12
  312.2 59.7 %all-reduce.26.cloned.1.call-done = (f32[256,256]{1,0:T(8,128)}, f32[256,256]{1,0:T(8,128)}, f32[1024,256]{1,0:T(8,128)}) async-done(((f32[256,256]{1,0:T(8,128)}, f32[256,256]{1,0:T(8,128)}, f32[1024,256]{1,0:T(8,128)}), (f32[256,256]{1,0:T(8,128)}, f32[256,256]{1,0:T(8,128)}, f32[1024,256]{1,0:T(8,128)})) %all-reduce.26.cloned.1.call-update) | async-done | bytes 1572880 | tf_op jit(solution)/shard_map/psum | solution.py:53
  378.3 11.7 %cholesky.248 = f32[128,128]{1,0:T(8,128)S(1)} custom-call(f32[128,128]{1,0:T(8,128)S(1)} %cholesky.349), custom_call_target="Cholesky" | custom-call | tf_op jit(solution)/shard_map/jit(cholesky)/cholesky | solution.py:60
  390.6 9.8 %custom-call.34 = f32[1,128,128]{1,2,0:T(8,128)S(1)} custom-call(f32[1,128,128]{2,1,0:T(8,128)S(1)} %get-tuple-element.199), custom_call_target="InvertDiagBlocksLowerTriangular" | custom-call | tf_op jit(solution)/shard_map/jit(cholesky)/cholesky | solution.py:60
  402.5 11.7 %cholesky.265 = f32[128,128]{1,0:T(8,128)S(1)} custom-call(f32[128,128]{1,0:T(8,128)S(1)} %convolution_subtract_fusion.16), custom_call_target="Cholesky" | custom-call | tf_op jit(solution)/shard_map/jit(cholesky)/cholesky | solution.py:60
  418.5 5.3 while.27
  419.8 1.4 bitcast_dynamic-update-slice_fusion.9
  422.4 1.4 bitcast_dynamic-update-slice_fusion.9
  424.5 20.9 %custom-call.35 = f32[2,128,128]{1,2,0:T(8,128)S(1)} custom-call(f32[2,128,128]{2,1,0:T(8,128)} %copy-done.29), custom_call_target="InvertDiagBlocksLowerTriangular" | custom-call | tf_op jit(solution)/shard_map/jit(_cho_solve)/triangular_solve | solution.py:60
  450.0 1.6 fusion.32
  451.6 3.6 fusion.14
  455.2 3.6 fusion.5
  458.8 1.8 fusion.21
  460.6 4.2 convolution_subtract_fusion.1
  464.9 3.5 fusion.3
  468.5 3.2 convolution_subtract_fusion.5
  471.8 2.0 fusion.20
  473.8 9.3 fusion.202
  483.1 50.4 %all-reduce.18.cloned.1.call-done = f32[2048,256]{0,1:T(8,128)} async-done(((f32[2048,256]{0,1:T(8,128)}), f32[2048,256]{0,1:T(8,128)}) %all-reduce.18.cloned.1.call-update) | async-done | bytes 2097168 | tf_op jit(solution)/shard_map/psum | solution.py:14
  533.5 4.8 fusion.203
  538.4 13.5 %subtract_subtract_fusion.1 = f32[2048,1024]{0,1:T(8,128)} fusion(f32[2048,1024]{0,1:T(8,128)} %copy.39, f32[2048,1024]{0,1:T(8,128)} %fusion.202, f32[2048,256]{0,1:T(8,128)S(1)} %fusion.6, f32[1024,256]{1,0:T(8,128)S(1)} %copy-done.8), kind=kOutput, calls=%fused_computation.9 | convolution fusion | flops 6446645248 | bytes 28311552 | tf_op jit(solution)/shard_map/dot_general | solution.py:18
  552.0 4.8 fusion.4
  556.8 3.4 fusion.17
  560.9 34.0 %all-reduce.24.cloned.1.call-done = (f32[256,1024]{0,1:T(8,128)}, f32[256,256]{0,1:T(8,128)}) async-done(((f32[256,1024]{0,1:T(8,128)}, f32[256,256]{0,1:T(8,128)}), (f32[256,1024]{0,1:T(8,128)}, f32[256,256]{0,1:T(8,128)})) %all-reduce.24.cloned.1.call-update) | async-done | bytes 1310736 | tf_op jit(solution)/shard_map/psum | solution.py:14
  597.7 11.7 %cholesky.282 = f32[128,128]{1,0:T(8,128)S(1)} custom-call(f32[128,128]{1,0:T(8,128)S(1)} %cholesky.352), custom_call_target="Cholesky" | custom-call | tf_op jit(solution)/shard_map/jit(cholesky)/cholesky | solution.py:54
  610.0 9.8 %custom-call.38 = f32[1,128,128]{1,2,0:T(8,128)S(1)} custom-call(f32[1,128,128]{2,1,0:T(8,128)S(1)} %get-tuple-element.195), custom_call_target="InvertDiagBlocksLowerTriangular" | custom-call | tf_op jit(solution)/shard_map/jit(cholesky)/cholesky | solution.py:54
  622.0 11.9 %cholesky.299 = f32[128,128]{1,0:T(8,128)S(1)} custom-call(f32[128,128]{1,0:T(8,128)S(1)} %convolution_subtract_fusion.15), custom_call_target="Cholesky" | custom-call | tf_op jit(solution)/shard_map/jit(cholesky)/cholesky | solution.py:54
  638.1 5.1 while.28
  643.9 20.5 %custom-call.39 = f32[2,128,128]{1,2,0:T(8,128)S(1)} custom-call(f32[2,128,128]{2,1,0:T(8,128)} %copy-done.30), custom_call_target="InvertDiagBlocksLowerTriangular" | custom-call | tf_op jit(solution)/shard_map/jit(_solve_triangular)/triangular_solve | solution.py:56
  667.6 11.1 %fusion.56 = f32[2048,256]{0,1:T(8,128)} fusion(f32[2048,1024]{0,1:T(8,128)} %fusion.17, f32[128,1024]{1,0:T(8,128)S(1)} %fusion.137, f32[128,1024]{1,0:T(8,128)S(1)} %fusion.43, s32[1024]{0:T(1024)S(1)} %broadcast_add_fusion.2), kind=kOutput, calls=%fused_computation.102 | convolution fusion | flops 6443499520 | bytes 11538432 | tf_op jit(solution)/shard_map/dot_general | solution.py:18
  681.9 10.5 %fusion.80 = f32[1024,256]{1,0:T(8,128)} fusion(f32[2048,1024]{0,1:T(8,128)} %fusion.17, f32[128,2048]{1,0:T(8,128)S(1)} %fusion.135, f32[128,2048]{1,0:T(8,128)S(1)} %fusion.22, s32[2048]{0:T(1024)S(1)} %broadcast_add_fusion), kind=kOutput, calls=%fused_computation.144 | convolution fusion | flops 6444548096 | bytes 11542528 | tf_op jit(solution)/shard_map/dot_general | solution.py:18
  692.4 51.4 %all-reduce.20.cloned.1.call-done = f32[2048,256]{0,1:T(8,128)} async-done(((f32[2048,256]{0,1:T(8,128)}), f32[2048,256]{0,1:T(8,128)}) %all-reduce.20.cloned.1.call-update) | async-done | bytes 2097168 | tf_op jit(solution)/shard_map/psum | solution.py:65
  743.8 4.5 fusion.8
  748.3 61.2 %all-reduce.22.cloned.1.call-done = (f32[256,256]{1,0:T(8,128)}, f32[256,256]{1,0:T(8,128)}, f32[1024,256]{1,0:T(8,128)}) async-done(((f32[256,256]{1,0:T(8,128)}, f32[256,256]{1,0:T(8,128)}, f32[1024,256]{1,0:T(8,128)}), (f32[256,256]{1,0:T(8,128)}, f32[256,256]{1,0:T(8,128)}, f32[1024,256]{1,0:T(8,128)})) %all-reduce.22.cloned.1.call-update) | async-done | bytes 1572880 | tf_op jit(solution)/shard_map/psum | solution.py:53
  812.8 11.7 %cholesky.316 = f32[128,128]{1,0:T(8,128)S(1)} custom-call(f32[128,128]{1,0:T(8,128)S(1)} %cholesky.355), custom_call_target="Cholesky" | custom-call | tf_op jit(solution)/shard_map/jit(cholesky)/cholesky | solution.py:60
  824.5 9.8 %custom-call.41 = f32[1,128,128]{1,2,0:T(8,128)S(1)} custom-call(f32[1,128,128]{2,1,0:T(8,128)S(1)} %get-tuple-element.191), custom_call_target="InvertDiagBlocksLowerTriangular" | custom-call | tf_op jit(solution)/shard_map/jit(cholesky)/cholesky | solution.py:60
  834.8 11.9 %cholesky.333 = f32[128,128]{1,0:T(8,128)S(1)} custom-call(f32[128,128]{1,0:T(8,128)S(1)} %convolution_subtract_fusion.14), custom_call_target="Cholesky" | custom-call | tf_op jit(solution)/shard_map/jit(cholesky)/cholesky | solution.py:60
  849.5 5.2 while.29
  850.7 1.4 bitcast_dynamic-update-slice_fusion.11
  854.7 19.7 %custom-call.42 = f32[2,128,128]{1,2,0:T(8,128)S(1)} custom-call(f32[2,128,128]{2,1,0:T(8,128)S(1)} %get-tuple-element.135), custom_call_target="InvertDiagBlocksLowerTriangular" | custom-call | tf_op jit(solution)/shard_map/jit(_cho_solve)/triangular_solve | solution.py:60
  877.0 3.5 fusion.10
  880.5 3.5 fusion.1
  884.0 7.1 fusion.54
  892.1 1.8 fusion.18
  894.0 10.2 %subtract_subtract_fusion = f32[2048,1024]{0,1:T(8,128)S(1)} fusion(f32[2048,1024]{0,1:T(8,128)} %fusion.17, f32[2048,1024]{0,1:T(8,128)S(1)} %fusion.54, f32[1024,256]{1,0:T(8,128)S(1)} %fusion.18, f32[128,2048]{1,0:T(8,128)S(1)} %fusion.135, f32[128,2048]{1,0:T(8,128)S(1)} %fusion.22, s32[2048]{0:T(1024)S(1)} %broadcast_add_fusion), kind=kOutput, calls=%fused_computation.8 | convolution fusion | flops 6448742400 | bytes 28319744 | tf_op jit(solution)/shard_map/dot_general | solution.py:18
  904.2 2.3 fusion
  907.7 7.3 copy.41
  915.1 8.0 copy.23
  (224 shorter events, 79.3 us)
Async XLA Ops:
  6.5 89.1 %all-reduce.14.cloned.1.call-start = ((), (), s32[]{:S(2)}) async-start(), calls=%async_computation | async-start | bytes 4194304 | tf_op jit(solution)/shard_map/psum | solution.py:14
  24.6 281.9 %copy-start.31 = (pred[2048]{0:T(1024)(128)(4,1)}, pred[2048]{0:T(1024)(128)(4,1)S(1)}, u32[]{:S(2)}) copy-start(pred[2048]{0:T(1024)(128)(4,1)S(1)} %broadcast_compare_fusion.1) | copy-start | bytes 6148
  28.0 129.2 %all-reduce.28.cloned.1.call-start = ((), (), s32[]{:S(2)}) async-start(), calls=%async_computation.7 | async-start | bytes 2621440 | tf_op jit(solution)/shard_map/psum | solution.py:14
  29.8 1.4 copy-start.9
  29.8 1.3 copy-start.40
  95.7 5.8 copy-start.3
  100.6 205.9 %all-reduce.16.cloned.1.call-start = ((), (), s32[]{:S(2)}) async-start(), calls=%async_computation.1 | async-start | bytes 4194304 | tf_op jit(solution)/shard_map/psum | solution.py:65
  101.4 129.2 %copy-start.36 = (s32[1024]{0:T(1024)}, s32[1024]{0:T(1024)S(1)}, u32[]{:S(2)}) copy-start(s32[1024]{0:T(1024)S(1)} %broadcast_add_fusion.3) | copy-start | bytes 12292
  101.5 143.2 %copy-start.34 = (s32[2048]{0:T(1024)}, s32[2048]{0:T(1024)S(1)}, u32[]{:S(2)}) copy-start(s32[2048]{0:T(1024)S(1)} %broadcast_add_fusion.1) | copy-start | bytes 24580
  157.1 70.1 %copy-start.15 = (f32[256,1024]{0,1:T(8,128)S(1)}, f32[256,1024]{0,1:T(8,128)}, u32[]{:S(2)}) copy-start(f32[256,1024]{0,1:T(8,128)} %get-tuple-element.178) | copy-start | bytes 3145732
  159.3 0.7 copy-start.23
  196.0 2.5 copy-start.16
  206.1 0.7 copy-start.28
  241.4 130.5 %all-reduce.26.cloned.1.call-start = ((), (), s32[]{:S(2)}) async-start(), calls=%async_computation.6 | async-start | bytes 3145728 | tf_op jit(solution)/shard_map/psum | solution.py:53
  310.8 222.8 %all-reduce.18.cloned.1.call-start = ((), (), s32[]{:S(2)}) async-start(), calls=%async_computation.2 | async-start | bytes 4194304 | tf_op jit(solution)/shard_map/psum | solution.py:14
  377.6 0.7 copy-start.24
  415.6 1.9 copy-start.18
  423.9 0.7 copy-start.29
  445.4 3.7 copy-start.26
  445.4 4.5 copy-start.21
  448.8 2.8 copy-start.10
  448.8 2.8 copy-start.32
  458.8 6.1 copy-start
  460.6 4.3 copy-start.6
  468.5 3.3 copy-start.38
  468.5 126.4 %all-reduce.24.cloned.1.call-start = ((), (), s32[]{:S(2)}) async-start(), calls=%async_computation.5 | async-start | bytes 2621440 | tf_op jit(solution)/shard_map/psum | solution.py:14
  468.5 3.2 copy-start.7
  471.8 2.1 copy-start.1
  483.1 55.3 %copy-start.8 = (f32[1024,256]{1,0:T(8,128)S(1)}, f32[1024,256]{1,0:T(8,128)}, u32[]{:S(2)}) copy-start(f32[1024,256]{1,0:T(8,128)} %copy-done.6) | copy-start | bytes 3145732
  538.4 13.6 %copy-start.17 = (f32[256,256]{1,0:T(8,128)S(1)}, f32[256,256]{1,0:T(8,128)}, u32[]{:S(2)}) copy-start(f32[256,256]{1,0:T(8,128)} %copy-done.16) | copy-start | bytes 786436
  538.4 13.6 %copy-start.33 = (pred[2048]{0:T(1024)(128)(4,1)S(1)}, pred[2048]{0:T(1024)(128)(4,1)}, u32[]{:S(2)}) copy-start(pred[2048]{0:T(1024)(128)(4,1)} %copy-done.31) | copy-start | bytes 6148
  538.4 13.6 %copy-start.35 = (s32[2048]{0:T(1024)S(1)}, s32[2048]{0:T(1024)}, u32[]{:S(2)}) copy-start(s32[2048]{0:T(1024)} %copy-done.34) | copy-start | bytes 24580
  538.4 205.4 %all-reduce.20.cloned.1.call-start = ((), (), s32[]{:S(2)}) async-start(), calls=%async_computation.3 | async-start | bytes 4194304 | tf_op jit(solution)/shard_map/psum | solution.py:65
  552.0 4.8 copy-start.37
  552.0 4.8 copy-start.41
  556.7 3.4 copy-start.2
  594.9 69.5 %copy-start.14 = (f32[256,1024]{0,1:T(8,128)S(1)}, f32[256,1024]{0,1:T(8,128)}, u32[]{:S(2)}) copy-start(f32[256,1024]{0,1:T(8,128)} %get-tuple-element.173) | copy-start | bytes 3145732
  597.0 0.7 copy-start.25
  635.2 1.9 copy-start.19
  643.3 0.7 copy-start.30
  665.1 1.7 copy-start.4
  666.7 0.8 copy-start.12
  678.7 130.7 %all-reduce.22.cloned.1.call-start = ((), (), s32[]{:S(2)}) async-start(), calls=%async_computation.4 | async-start | bytes 3145728 | tf_op jit(solution)/shard_map/psum | solution.py:53
  834.6 41.6 %copy-start.27 = (f32[256,256]{1,0:T(8,128)S(1)}, f32[256,256]{1,0:T(8,128)}, u32[]{:S(2)}) copy-start(f32[256,256]{1,0:T(8,128)} %get-tuple-element.171) | copy-start | bytes 786436
  874.4 2.6 copy-start.11
  880.4 3.5 copy-start.5
  880.5 3.5 copy-start.13
  884.0 7.1 copy-start.22
  884.0 7.1 copy-start.39
  894.0 10.2 %copy-start.20 = (f32[256,256]{1,0:T(8,128)S(1)}, f32[256,256]{1,0:T(8,128)}, u32[]{:S(2)}) copy-start(f32[256,256]{1,0:T(8,128)} %copy-done.19) | copy-start | bytes 786436
Sparse Core Ops, SparseCore 0:
  28.1 67.5 all-reduce.13
  100.7 56.3 all-reduce.27
  241.6 64.9 all-reduce.15
  310.9 60.9 all-reduce.25
  468.6 64.8 all-reduce.17
  538.5 56.3 all-reduce.23
  678.8 64.9 all-reduce.19
  748.4 60.9 all-reduce.21
where the time goes:
time: 937 us; the launch traced here: 930 us
  waiting for transfers between devices  421 us (45%)
  other arithmetic  238 us (25%)
  matrix products  184 us (20%)
  local copies, waits for them, and re-layouts  65.4 us (7%)
  between operations  20.2 us (2%)
    psum x4, waiting for transfers between devices, broadcast(): return lax.psum(jnp.where(mine, value, jnp.zeros_like(value)), axis)  204 us
    dot_general x34, matrix products, matmul(): jnp.dot(left, right, precision=highest, preferred_element_type=jnp.float32)  155 us
    psum x2, waiting for transfers between devices, shards(): lax.psum((matmul(low_rows.T, low_rows), top_part), 'row')  121 us
    psum x2, waiting for transfers between devices, shards(): applied_rows = lax.psum(matmul(dense, vec_cols), 'col')  96.3 us
    another operation x13, other arithmetic, shards(): factor = jnp.linalg.cholesky(gram_sum)  71 us
    another operation x14, other arithmetic, shards(): jnp.linalg.cholesky(normal)  70.6 us
    another operation x5, other arithmetic, shards(): jax.scipy.linalg.solve_triangular(factor, right_cols, lower=True)  43.5 us
    another operation x4, other arithmetic, shards(): jax.scipy.linalg.cho_solve((jnp.linalg.cholesky(normal), True), shifted.T)  41.6 us
  transfers between devices with their start and end apart: 8, of which 8 were waited for; matrix products, arithmetic and copies ran while one was open for 8% of the time, Pallas kernels for 0%

commit v1 on v0

v1 whole, which is shorter than its diff:
```python
import functools

import jax
import jax.numpy as jnp
from jax import lax
from jax.experimental import pallas as pl
from jax.experimental.pallas import tpu as pltpu
from jax.sharding import PartitionSpec as P

PANELS = 2
MESH = pl.DeviceIdType.MESH
VMEM = pl.BlockSpec(memory_space=pltpu.VMEM)
highest = lax.Precision.HIGHEST
high = lax.Precision.HIGH


def dot(left, right, precision=highest):
    return jnp.dot(left, right, precision=precision, preferred_element_type=jnp.float32)


def dot_tn(left, right):
    return lax.dot_general(left, right, (((0,), (0,)), ((), ())), precision=highest,
                           preferred_element_type=jnp.float32)


def dot_nt(left, right):
    return lax.dot_general(left, right, (((1,), (1,)), ((), ())), precision=highest,
                           preferred_element_type=jnp.float32)


def remote(src, dst, send, recv, row, col):
    return pltpu.make_async_remote_copy(src_ref=src, dst_ref=dst, send_sem=send, recv_sem=recv,
                                        device_id=(row, col), device_id_type=MESH)


def greet(devices):
    barrier = pltpu.get_barrier_semaphore()
    for cond, row, col in devices:
        def hail(row=row, col=col):
            pl.semaphore_signal(barrier, inc=1, device_id=(row, col), device_id_type=MESH)
        if cond is True:
            hail()
        else:
            pl.when(cond)(hail)
    heard = sum(1 if cond is True else cond.astype(jnp.int32) for cond, _, _ in devices)
    pl.semaphore_wait(barrier, heard)


def ring_place(row, rows):
    return row + (row // 2) * (5 - 2 * row) if rows == 4 else row


RING_CHUNKS = 4


def spread_kernel(panel, rows, cols, xr_in, xct_in, gram_in, top_in, xr, xct, gt, slots,
                  send_z, send_k, recv_z, send_a, recv_a, send_b, recv_b,
                  send_g, recv_g, send_t, recv_t):
    width = gram_in.shape[0]
    r, c = lax.axis_index("row"), lax.axis_index("col")
    z, k, chips = c // 2, c % 2, cols // 2
    root_row, root_col, top_row = panel % rows, panel % cols, (panel + 1) % rows
    core = root_col % 2
    assert root_col // 2 == 0
    blocks = xr.shape[0] // width
    place = ring_place(r, rows)
    after = ring_place((place + 1) % rows, rows)
    before = ring_place((place + rows - 1) % rows, rows)
    ahead = (place - ring_place(root_row, rows) + rows) % rows
    behind = (rows - ahead) % rows
    peers = [(r + i) % rows for i in range(1, rows)]
    greet([(True, peer, c) for peer in peers]
          + [(True, r, c + 1 - 2 * k), (z > 0, r, c - 2), (z < chips - 1, r, c + 2)])

    owner = c == root_col
    relay = k == core

    def z_piece(i):
        if i < blocks:
            return xr.at[pl.ds(i * width, width)]
        return gt.at[i - blocks]

    def to_chip(i):
        return remote(z_piece(i), z_piece(i), send_z.at[i], recv_z.at[i], r, c + 2)

    def to_core(i):
        return remote(z_piece(i), z_piece(i), send_k.at[i], recv_z.at[i], r, c + 1 - 2 * k)

    def forward(i):
        pl.when(z < chips - 1)(lambda: to_chip(i).start())
        to_core(i).start()

    def gram_to(i, peer):
        return remote(gram_in, slots.at[i - 1], send_g.at[i - 1], recv_g.at[i - 1], peer, c)

    def top_to(i, peer):
        return remote(gt.at[1], gt.at[1], send_t.at[i - 1], recv_t, peer, c)

    half = width // 2
    step = half // RING_CHUNKS

    def ring_piece(side, i):
        return xct.at[pl.ds(side * half + i * step, step)]

    def to_after(i):
        return remote(ring_piece(0, i), ring_piece(0, i), send_a.at[i], recv_a.at[i], after, c)

    def to_before(i):
        return remote(ring_piece(1, i), ring_piece(1, i), send_b.at[i], recv_b.at[i], before, c)

    @pl.when(owner)
    def _():
        for i, peer in enumerate(peers, 1):
            gram_to(i, peer).start()

        @pl.when(r == top_row)
        def _():
            gt[1] = top_in[...]
            for i, peer in enumerate(peers, 1):
                top_to(i, peer).start()

    @pl.when(ahead == 0)
    def _():
        xct[...] = xct_in[...]
        for i in range(RING_CHUNKS):
            to_after(i).start()
            to_before(i).start()

    @pl.when(owner)
    def _():
        for i in range(blocks):
            xr[pl.ds(i * width, width), :] = xr_in[pl.ds(i * width, width), :]
            forward(i)
        total = gram_in[...]
        for i, peer in enumerate(peers, 1):
            gram_to(i, peer).wait()
            total = total + slots[i - 1]
        gt[0] = total
        forward(blocks)

        @pl.when(r != top_row)
        def _():
            top_to(1, peers[0]).wait_recv()

        forward(blocks + 1)

    for i in range(max(blocks + 2, RING_CHUNKS)):
        if i < RING_CHUNKS:
            @pl.when(ahead != 0)
            def _(i=i):
                to_after(i).wait_recv()
                pl.when(ahead < rows - 1)(lambda: to_after(i).start())
                to_before(i).wait_recv()
                pl.when(behind < rows - 1)(lambda: to_before(i).start())
        if i < blocks + 2:
            @pl.when(jnp.logical_not(owner))
            def _(i=i):
                to_core(i).wait_recv()
                pl.when(relay)(lambda: forward(i))

    @pl.when(owner & (r == top_row))
    def _():
        for i, peer in enumerate(peers, 1):
            top_to(i, peer).wait_send()

    @pl.when(relay)
    def _():
        for i in range(blocks + 2):
            pl.when(z < chips - 1)(lambda: to_chip(i).wait_send())
            to_core(i).wait_send()

    for i in range(RING_CHUNKS):
        pl.when(ahead < rows - 1)(lambda: to_after(i).wait_send())
        pl.when(behind < rows - 1)(lambda: to_before(i).wait_send())


def spread(panel, rows, cols, xr, xct, gram, top):
    width = gram.shape[0]
    pieces = xr.shape[0] // width + 2
    dma = pltpu.SemaphoreType.DMA
    f32 = jnp.float32
    return pl.pallas_call(
        functools.partial(spread_kernel, panel, rows, cols),
        out_shape=(jax.ShapeDtypeStruct(xr.shape, f32), jax.ShapeDtypeStruct(xct.shape, f32),
                   jax.ShapeDtypeStruct((2, width, width), f32)),
        in_specs=[VMEM] * 4,
        out_specs=(VMEM,) * 3,
        scratch_shapes=[pltpu.VMEM((rows - 1, width, width), f32),
                        dma((pieces,)), dma((pieces,)), dma((pieces,)),
                        dma((RING_CHUNKS,)), dma((RING_CHUNKS,)), dma((RING_CHUNKS,)), dma((RING_CHUNKS,)),
                        dma((rows - 1,)), dma((rows - 1,)), dma((rows - 1,)), dma],
        compiler_params=pltpu.CompilerParams(collective_id=panel, has_side_effects=True,
                                             vmem_limit_bytes=40 * 2**20),
        name=f"spread_panel_{panel}",
    )(xr, xct, gram, top)


GROUP = 4


def eliminate(block):
    size = block.shape[0]
    row = lax.broadcasted_iota(jnp.int32, (size, size), 0)
    col = lax.broadcasted_iota(jnp.int32, (size, size), 1)
    eye = (row == col).astype(jnp.float32)
    work = jnp.concatenate([block, eye], axis=1)
    lane_rows = lax.broadcasted_iota(jnp.int32, work.shape, 0)
    for base in range(0, size, GROUP):
        columns = [jnp.broadcast_to(work[:, base + i:base + i + 1], work.shape) for i in range(GROUP)]
        pivots = [work[base + i:base + i + 1, :] for i in range(GROUP)]
        change = None
        for i in range(GROUP):
            at = base + i
            inverse = 1.0 / columns[i][at:at + 1, :]
            factor = jnp.where(lane_rows > at, columns[i] * inverse, 0.0)
            for l in range(i + 1, GROUP):
                columns[l] = columns[l] - factor * columns[l][at:at + 1, :]
                pivots[l] = pivots[l] - factor[base + l:base + l + 1, :] * pivots[i]
            term = factor * pivots[i]
            change = term if change is None else change + term
        work = work - change
    diagonal = jnp.sum(jnp.where(row == col, work[:, :size], 0.0), axis=1, keepdims=True)
    return jnp.where(row >= col, work[:, size:] * lax.rsqrt(diagonal), 0.0)


def factorize(work, size):
    width = work.shape[0]
    for start in range(0, width, size):
        stop = start + size
        inverse = eliminate(work[start:stop, start:stop])
        strip = dot(inverse, work[start:stop, :])
        work[start:stop, :] = strip
        if stop < width:
            work[stop:, :] = work[stop:, :] - dot_tn(strip[:, stop:width], strip)


def factor_kernel(gt, upper, lower_inverse, coupling, work):
    width = upper.shape[0]
    row = lax.broadcasted_iota(jnp.int32, (width, width), 0)
    col = lax.broadcasted_iota(jnp.int32, (width, width), 1)
    eye = (row == col).astype(jnp.float32)
    work[:, :width] = gt[0]
    work[:, width:] = eye
    factorize(work, 64)
    upper[...] = jnp.where(row <= col, work[:, :width], 0.0)
    inverse = work[:, width:]
    lower_inverse[...] = inverse
    shifted = eye + dot_nt(gt[1], inverse)
    work[:, :width] = dot_tn(shifted, shifted)
    work[:, width:] = eye
    factorize(work, 64)
    inverse = work[:, width:]
    coupling[...] = dot_tn(inverse, dot_nt(inverse, shifted))


def factors(panel, gt):
    width = gt.shape[1]
    square = jax.ShapeDtypeStruct((width, width), jnp.float32)
    return pl.pallas_call(
        factor_kernel,
        out_shape=(square,) * 3,
        in_specs=[VMEM],
        out_specs=(VMEM,) * 3,
        scratch_shapes=[pltpu.VMEM((width, 2 * width), jnp.float32)],
        compiler_params=pltpu.CompilerParams(vmem_limit_bytes=32 * 2**20),
        name=f"factors_{panel}",
    )(gt)


def product_kernel(rows, cols, part, wct, wrt, slots, send_s, recv_s, send_g, recv_g,
                   send_up, send_down, send_k, recv_z):
    r, c = lax.axis_index("row"), lax.axis_index("col")
    z, k, chips = c // 2, c % 2, cols // 2
    share = part.shape[0] // rows
    halves = cols // rows
    relay = k == r % 2
    peers = [(r + i) % rows for i in range(1, rows)]
    greet([(True, peer, c) for peer in peers]
          + [(True, r, c + 1 - 2 * k), (z > 0, r, c - 2), (z < chips - 1, r, c + 2)])

    def rows_of(q):
        return pl.ds(pl.multiple_of(q * share, share), share)

    def scatter(i):
        return remote(part.at[rows_of(peers[i - 1])], slots.at[i - 1], send_s.at[i - 1], recv_s.at[i - 1],
                      peers[i - 1], c)

    def gather(i):
        return remote(wct.at[rows_of(r)], wct.at[rows_of(r)], send_g.at[i - 1], recv_g.at[i - 1],
                      peers[i - 1], c)

    for i in range(1, rows):
        scatter(i).start()
    total = part[rows_of(r), :]
    for i in range(1, rows):
        scatter(i).wait_recv()
        total = total + slots[i - 1]
    wct[rows_of(r), :] = total
    for i in range(1, rows):
        gather(i).start()

    def origin(h):
        return (r + rows * h) // 2

    def piece(h, i):
        return wrt.at[h, rows_of((r + rows - i) % rows)]

    def up(h, i):
        return remote(piece(h, i), piece(h, i), send_up.at[h, i], recv_z.at[h, i], r, c + 2)

    def down(h, i):
        return remote(piece(h, i), piece(h, i), send_down.at[h, i], recv_z.at[h, i], r, c - 2)

    def across(h, i):
        return remote(piece(h, i), piece(h, i), send_k.at[h, i], recv_z.at[h, i], r, c + 1 - 2 * k)

    for i in range(rows):
        if i:
            gather(i).wait_recv()
        for h in range(halves):
            @pl.when(c == r + rows * h)
            def _(h=h, i=i):
                place = rows_of((r + rows - i) % rows)
                wrt[h, place, :] = wct[place, :]
                pl.when(z < chips - 1)(lambda: up(h, i).start())
                pl.when(z > 0)(lambda: down(h, i).start())
                across(h, i).start()

    for i in range(rows):
        for h in range(halves):
            @pl.when(c != r + rows * h)
            def _(h=h, i=i):
                across(h, i).wait_recv()

                @pl.when(relay)
                def _():
                    pl.when((z > origin(h)) & (z < chips - 1))(lambda: up(h, i).start())
                    pl.when((z < origin(h)) & (z > 0))(lambda: down(h, i).start())
                    across(h, i).start()

    for i in range(1, rows):
        scatter(i).wait_send()
        gather(i).wait_send()

    @pl.when(relay)
    def _():
        for i in range(rows):
            for h in range(halves):
                pl.when((z >= origin(h)) & (z < chips - 1))(lambda: up(h, i).wait_send())
                pl.when((z <= origin(h)) & (z > 0))(lambda: down(h, i).wait_send())
                across(h, i).wait_send()


def reduce_product(panel, rows, cols, part):
    width, local_cols = part.shape
    halves = cols // rows
    dma = pltpu.SemaphoreType.DMA
    f32 = jnp.float32
    return pl.pallas_call(
        functools.partial(product_kernel, rows, cols),
        out_shape=(jax.ShapeDtypeStruct(part.shape, f32),
                   jax.ShapeDtypeStruct((halves, width, local_cols), f32)),
        in_specs=[VMEM],
        out_specs=(VMEM,) * 2,
        scratch_shapes=[pltpu.VMEM((rows - 1, width // rows, local_cols), f32),
                        dma((rows - 1,)), dma((rows - 1,)), dma((rows - 1,)), dma((rows - 1,)),
                        dma((halves, rows)), dma((halves, rows)), dma((halves, rows)), dma((halves, rows))],
        compiler_params=pltpu.CompilerParams(collective_id=PANELS + panel, has_side_effects=True,
                                             vmem_limit_bytes=40 * 2**20),
        name=f"reduce_product_{panel}",
    )(part)


def sum_kernel(rows, part, out, slots, send_s, recv_s, send_k, recv_k):
    r, c = lax.axis_index("row"), lax.axis_index("col")
    k = c % 2
    half = part.shape[0] // 2
    peers = [(r + i) % rows for i in range(1, rows)]
    greet([(True, peer, c) for peer in peers] + [(True, r, c + 1 - 2 * k)])
    mine = pl.ds(pl.multiple_of(k * half, half), half)

    def send(i):
        return remote(part.at[mine], slots.at[i - 1], send_s.at[i - 1], recv_s.at[i - 1], peers[i - 1], c)

    for i in range(1, rows):
        send(i).start()
    total = part[mine, :]
    for i in range(1, rows):
        send(i).wait()
        total = total + slots[i - 1]
    out[mine, :] = total
    swap = remote(out.at[mine], out.at[mine], send_k, recv_k, r, c + 1 - 2 * k)
    swap.start()
    swap.wait()


def sum_rows(panel, rows, part):
    dma = pltpu.SemaphoreType.DMA
    return pl.pallas_call(
        functools.partial(sum_kernel, rows),
        out_shape=jax.ShapeDtypeStruct(part.shape, jnp.float32),
        in_specs=[VMEM],
        out_specs=VMEM,
        scratch_shapes=[pltpu.VMEM((rows - 1, part.shape[0] // 2, part.shape[1]), jnp.float32),
                        dma((rows - 1,)), dma((rows - 1,)), dma, dma],
        compiler_params=pltpu.CompilerParams(collective_id=2 * PANELS + panel, has_side_effects=True,
                                             vmem_limit_bytes=32 * 2**20),
        name=f"sum_inner_{panel}",
    )(part)


def shards(matrix):
    row_blocks, width, col_blocks, _ = matrix.shape
    rows, cols = lax.axis_size("row"), lax.axis_size("col")
    halves = cols // rows
    row_index, col_index = lax.axis_index("row"), lax.axis_index("col")
    local_rows, local_cols = row_blocks * width, col_blocks * width
    dense = matrix.reshape(local_rows, local_cols)
    row_range = jnp.arange(local_rows, dtype=jnp.int32)
    col_range = jnp.arange(local_cols, dtype=jnp.int32)
    global_rows = (row_range // width * rows + row_index) * width + row_range % width
    global_cols = (col_range // width * cols + col_index) * width + col_range % width
    unit = jnp.arange(width, dtype=jnp.int32)
    for panel in range(PANELS):
        start = (panel + 1) * width
        col_slot, row_slot = panel // cols * width, panel // rows * width
        below = global_rows[:, None] >= start
        beside = global_cols[None, :] >= start
        low = jnp.where(below, dense[:, col_slot:col_slot + width], 0.0)
        right = jnp.where(beside, dense[row_slot:row_slot + width, :], 0.0)
        top_slot = (panel + 1) // rows * width
        xr, xct, gt = spread(panel, rows, cols, low, right, dot_tn(low, low),
                             low[top_slot:top_slot + width])
        upper, lower_inverse, coupling = factors(panel, gt)
        placed_rows = (global_rows[:, None] - start == unit[None, :]).astype(jnp.float32)
        placed_cols = (global_cols[None, :] - start == unit[:, None]).astype(jnp.float32)
        vec_rows = dot_nt(xr, lower_inverse) + placed_rows
        vec_cols = dot(lower_inverse, xct) + placed_cols
        part = lax.dot_general(vec_rows, dense, (((0,), (0,)), ((), ())), precision=high,
                               preferred_element_type=jnp.float32)
        part = jnp.where(beside, part, 0.0)
        applied_cols, applied = reduce_product(panel, rows, cols, part)
        applied = applied.reshape(halves, width, col_blocks, width)
        applied_rows = applied.transpose(2, 0, 3, 1).reshape(local_rows, width)
        inner = sum_rows(panel, rows, dot_tn(vec_rows, applied_rows))
        middle = dot_nt(dot(coupling, inner), coupling)
        factor_rows = dot_nt(applied_rows, coupling) - 0.5 * dot(vec_rows, middle)
        factor_cols = dot(coupling, applied_cols) - 0.5 * dot_tn(middle, vec_cols)
        dense = dense - dot(jnp.concatenate([factor_rows, vec_rows], axis=1),
                            jnp.concatenate([vec_cols, factor_cols], axis=0), high)
        old_col = dense[:, col_slot:col_slot + width]
        tiled = jnp.tile(-upper, (row_blocks, 1))
        on_top = (global_rows >= start) & (global_rows < start + width)
        new_col = jnp.where(below, jnp.where(on_top[:, None], tiled, 0.0), old_col)
        dense = dense.at[:, col_slot:col_slot + width].set(
            jnp.where(col_index == panel % cols, new_col, old_col))
        old_row = dense[row_slot:row_slot + width, :]
        tiled = jnp.tile(-upper.T, (1, col_blocks))
        on_top = (global_cols >= start) & (global_cols < start + width)
        new_row = jnp.where(beside, jnp.where(on_top[None, :], tiled, 0.0), old_row)
        dense = dense.at[row_slot:row_slot + width, :].set(
            jnp.where(row_index == panel % rows, new_row, old_row))
    return dense.reshape(matrix.shape)


def solution(mesh):
    assert mesh.shape["col"] % mesh.shape["row"] == 0 and mesh.shape["row"] % 2 == 0
    spec = P(None, "row", None, "col")
    return jax.shard_map(shards, mesh=mesh, in_specs=(spec,), out_specs=spec, check_vma=False)
```

time: 937 us -> 489 us (0.52)
  waiting for transfers between devices: 421 us -> 0 us
  Pallas kernels: 0 us -> 371 us
  other arithmetic: 238 us -> 16.7 us
  matrix products: 184 us -> 62.4 us
  local copies, waits for them, and re-layouts: 65.4 us -> 32.2 us
  between operations: 20.2 us -> 1.12 us
    psum x8 -> x0, waiting for transfers between devices: 421 us -> none  [the longest x4 204 us: broadcast(): return lax.psum(jnp.where(mine, value, jnp.zeros_like(value)), axis)]
    pallas_call x0 -> x8, Pallas kernels: none -> 371 us  [the longest x2 174 us: reduce_product(): pl.pallas_call(functools.partial(product_kernel, rows, cols), out_shape=(...]
    another operation x37 -> x1, other arithmetic: 227 us -> 0.69 us  [the longest x13 71 us: shards(): factor = jnp.linalg.cholesky(gram_sum)]
    dot_general x34 -> x24, matrix products: 155 us -> 62.4 us  [the longest x10 32.5 us: dot(): jnp.dot(left, right, precision=precision, preferred_element_type=jnp.floa...]
    another operation x38 -> x0, matrix products: 29.4 us -> none  [the longest x6 6.23 us: shards(): jax.scipy.linalg.solve_triangular(factor, low_rows.T, lower=True)]
    another operation x37 -> x2, local copies, waits for them, and re-layouts: 21.9 us -> 0.36 us  [shards(): tiled = jnp.tile(-upper.T, (1, col_blocks))]
    scatter x0 -> x3, other arithmetic: none -> 9.56 us  [the longest x2 7.17 us: shards(): dense.at[:, col_slot:col_slot + width]]
    unnamed x86 -> x36, local copies, waits for them, and re-layouts: 21.2 us -> 11.8 us
  transfers between devices with their start and end apart: 8 -> 0, of which waited for: 8 -> 0; matrix products, arithmetic and copies ran while one was open for 8% -> 0% of each run, Pallas kernels for 0% -> 0%
where the time goes in v1:
time: 489 us; the launch traced here: 483 us
  Pallas kernels  371 us (76%)
  matrix products  62.4 us (13%)
  local copies, waits for them, and re-layouts  32.2 us (7%)
  other arithmetic  16.7 us (3%)
    pallas_call x2, Pallas kernels, reduce_product(): pl.pallas_call(functools.partial(product_kernel, rows, cols), out_shape=(...  174 us
    pallas_call x2, Pallas kernels, spread(): pl.pallas_call(functools.partial(spread_kernel, panel, rows, cols), out_s...  101 us
    pallas_call x2, Pallas kernels, factors(): pl.pallas_call(factor_kernel, out_shape=(square,) * 3, in_specs=[VMEM], o...  60.1 us
    pallas_call x2, Pallas kernels, sum_rows(): pl.pallas_call(functools.partial(sum_kernel, rows), out_shape=jax.ShapeDt...  35.8 us
    dot_general x10, matrix products, dot(): jnp.dot(left, right, precision=precision, preferred_element_type=jnp.floa...  32.5 us
    dot_general x6, matrix products, dot_tn(): lax.dot_general(left, right, (((0,), (0,)), ((), ())), precision=highest,...  12.8 us
    unnamed x36, local copies, waits for them, and re-layouts  11.8 us
    reshape x1, local copies, waits for them, and re-layouts, shards(): return dense.reshape(matrix.shape)  10.5 us

profile of v1, /device:TPU:0, one launch (start us, length us, event | category | flops | bytes accessed | tf_op | source)
XLA Modules:
  0.0 483.4 jit_solution(986812162761334765)
XLA Ops:
  0.0 8.9 %copy.8 = f32[256,8,4,256]{3,1,2,0:T(8,128)} copy(f32[256,8,4,256]{3,2,1,0:T(4,128)} %bitcast.79) | data formatting | bytes 16777216
  8.9 1.8 slice_select_fusion.1.xr_in
  10.7 1.4 slice.100
  12.1 0.2 copy.9
  12.3 0.0 slice-start.2
  12.3 0.1 broadcast_select_fusion.1.xct_in
  12.4 3.5 fusion.52.gram_in
  15.9 0.0 slice-start.3
  16.0 33.8 %spread_panel_0.1 = (f32[2048,256]{1,0:T(8,128)S(1)}, f32[256,1024]{1,0:T(8,128)S(1)}, f32[2,256,256]{2,1,0:T(8,128)S(1)}) custom-call(f32[2048,256]{1,0:T(8,128)S(1)} %slice_select_fusion.1.xr_in, f32[256,1024]{1,0:T(8,128)S(1)} %broadcast_select_fusion.1.xct_in, f32[256,256]{1,0:T(8,128)S(1)} %fusion.52.gram_in, f32[256,256]{1,0:T(8,128)S(1)} %slice.110.top_in), custom_call_target="tpu_custom_call" | custom-call | tf_op jit(solution)/shard_map/spread_panel_0/pallas_call | solution.py:182
  49.8 30.1 %factors_0.1 = (f32[256,256]{1,0:T(8,128)S(1)}, f32[256,256]{1,0:T(8,128)S(1)}, f32[256,256]{1,0:T(8,128)S(1)}) custom-call(f32[2,256,256]{2,1,0:T(8,128)S(1)} %get-tuple-element.70.gt), custom_call_target="tpu_custom_call" | custom-call | tf_op jit(solution)/shard_map/factors_0/pallas_call | solution.py:259
  79.8 2.1 convolution_add_fusion.1
  82.0 4.0 convolution_select_fusion.1.part
  86.0 117.9 %reduce_product_0.1 = (f32[256,1024]{1,0:T(8,128)S(1)}, f32[2,256,1024]{2,1,0:T(8,128)S(1)}) custom-call(f32[256,1024]{1,0:T(8,128)S(1)} %convolution_select_fusion.1.part), custom_call_target="tpu_custom_call" | custom-call | tf_op jit(solution)/shard_map/reduce_product_0/pallas_call | solution.py:359
  203.9 1.0 copy-done.4
  204.9 2.0 reshape.223
  206.9 1.9 copy.4
  208.8 0.0 copy-start.9
  208.8 2.0 fusion.53
  210.8 1.9 fusion.54.part
  212.7 18.9 %sum_inner_0.1 = f32[256,256]{1,0:T(8,128)S(1)} custom-call(f32[256,256]{1,0:T(8,128)S(1)} %fusion.54.part), custom_call_target="tpu_custom_call" | custom-call | tf_op jit(solution)/shard_map/sum_inner_0/pallas_call | solution.py:399
  231.6 0.4 fusion.55
  232.0 0.4 fusion.56
  232.4 0.0 copy-start.5
  232.4 2.1 fusion.15
  234.6 1.0 fusion.57
  235.6 0.2 copy-done.1
  235.8 1.1 convolution_add_fusion.3
  236.9 1.0 fusion.25
  237.9 11.7 %fusion.11 = f32[2048,1024]{1,0:T(8,128)} fusion(f32[2048,1024]{1,0:T(8,128)} %bitcast.71, f32[2048,256]{0,1:T(8,128)S(1)} %copy-done.9, f32[2048,256]{0,1:T(8,128)S(1)} %fusion.15, f32[256,1024]{1,0:T(8,128)S(1)} %fusion.25, f32[256,1024]{1,0:T(8,128)S(1)} %convolution_add_fusion.3), kind=kOutput, calls=%fused_computation.9 | convolution fusion | flops 6446120960 | bytes 23068672 | tf_op jit(solution)/shard_map/dot_general | solution.py:18
  249.6 0.7 compare_reduce_fusion
  250.4 3.5 fusion.16
  253.9 0.1 copy.5
  254.1 0.2 tile.18
  254.2 0.2 copy.10
  254.5 2.5 broadcast_select_fusion
  257.0 1.9 slice_select_fusion.xr_in
  258.9 3.5 fusion.58.gram_in
  262.4 0.0 slice-start.1
  262.5 67.4 %spread_panel_1.1 = (f32[2048,256]{1,0:T(8,128)S(1)}, f32[256,1024]{1,0:T(8,128)S(1)}, f32[2,256,256]{2,1,0:T(8,128)S(1)}) custom-call(f32[2048,256]{1,0:T(8,128)S(1)} %slice_select_fusion.xr_in, f32[256,1024]{1,0:T(8,128)S(1)} %get-tuple-element.85.xct_in, f32[256,256]{1,0:T(8,128)S(1)} %fusion.58.gram_in, f32[256,256]{1,0:T(8,128)S(1)} %slice.114.top_in), custom_call_target="tpu_custom_call" | custom-call | tf_op jit(solution)/shard_map/spread_panel_1/pallas_call | solution.py:182
  329.9 0.0 copy-start.2
  329.9 30.1 %factors_1.1 = (f32[256,256]{1,0:T(8,128)S(1)}, f32[256,256]{1,0:T(8,128)S(1)}, f32[256,256]{1,0:T(8,128)S(1)}) custom-call(f32[2,256,256]{2,1,0:T(8,128)S(1)} %get-tuple-element.78.gt), custom_call_target="tpu_custom_call" | custom-call | tf_op jit(solution)/shard_map/factors_1/pallas_call | solution.py:259
  360.0 2.1 convolution_add_fusion
  362.2 4.0 convolution_select_fusion.part
  366.2 55.9 %reduce_product_1.1 = (f32[256,1024]{1,0:T(8,128)S(1)}, f32[2,256,1024]{2,1,0:T(8,128)S(1)}) custom-call(f32[256,1024]{1,0:T(8,128)S(1)} %convolution_select_fusion.part), custom_call_target="tpu_custom_call" | custom-call | tf_op jit(solution)/shard_map/reduce_product_1/pallas_call | solution.py:359
  422.1 1.0 copy-done.6
  423.0 2.0 reshape.225
  425.0 1.9 copy.6
  427.0 2.0 fusion.59
  429.0 1.9 fusion.60.part
  430.9 16.9 %sum_inner_1.1 = f32[256,256]{1,0:T(8,128)S(1)} custom-call(f32[256,256]{1,0:T(8,128)S(1)} %fusion.60.part), custom_call_target="tpu_custom_call" | custom-call | tf_op jit(solution)/shard_map/sum_inner_1/pallas_call | solution.py:399
  447.8 0.4 fusion.61
  448.2 0.4 fusion.62
  448.6 2.1 fusion.14
  450.7 1.0 fusion.63
  451.8 0.2 copy-done.3
  452.0 1.1 convolution_add_fusion.2
  453.0 1.0 fusion.24
  454.1 11.6 %fusion.8 = f32[2048,1024]{1,0:T(8,128)} fusion(f32[2048,1024]{1,0:T(8,128)} %get-tuple-element.86, f32[2048,256]{0,1:T(8,128)S(1)} %copy-done.11, f32[2048,256]{0,1:T(8,128)S(1)} %fusion.14, f32[256,1024]{1,0:T(8,128)S(1)} %fusion.24, f32[256,1024]{1,0:T(8,128)S(1)} %convolution_add_fusion.2), kind=kOutput, calls=%fused_computation.8 | convolution fusion | flops 6446120960 | bytes 23068672 | tf_op jit(solution)/shard_map/dot_general | solution.py:18
  465.8 3.6 fusion.17
  469.4 0.1 copy.7
  469.5 0.2 tile.42
  469.7 0.2 copy.11
  469.9 2.4 fusion.26
  472.3 10.5 %reshape.227 = f32[8,256,4,256]{3,2,1,0:T(4,128)} reshape(f32[2048,1024]{1,0:T(8,128)} %fusion.26) | data formatting | bytes 16777216 | tf_op jit(solution)/shard_map/reshape | solution.py:463
  (34 shorter events, 0.2 us)
Async XLA Ops:
  12.3 69.7 %slice-start.2 = ((s8[8388608]{0:T(1024)(128)(4,1)}), s8[4194304]{0:T(1024)(128)(4,1)S(1)}, s32[]{:S(2)}) async-start(s8[8388608]{0:T(1024)(128)(4,1)} %bitcast.72), calls=%async_computation.2 | async-start | bytes 8388608
  15.9 66.1 %slice-start.3 = ((s8[8388608]{0:T(1024)(128)(4,1)}), s8[4194304]{0:T(1024)(128)(4,1)S(1)}, s32[]{:S(2)}) async-start(s8[8388608]{0:T(1024)(128)(4,1)} %bitcast.72), calls=%async_computation.3 | async-start | bytes 8388608
  49.8 32.2 %copy-start = (f32[256,1024]{1,0:T(8,128)}, f32[256,1024]{1,0:T(8,128)S(1)}, u32[]{:S(2)}) copy-start(f32[256,1024]{1,0:T(8,128)S(1)} %get-tuple-element.74) | copy-start | bytes 3145732
  82.0 4.0 copy-start.8
  203.9 1.0 copy-start.4
  208.8 2.0 copy-start.9
  232.4 2.1 copy-start.5
  234.5 1.2 copy-start.1
  257.0 105.1 %slice-start = ((s8[8388608]{0:T(1024)(128)(4,1)}), s8[4194304]{0:T(1024)(128)(4,1)S(1)}, s32[]{:S(2)}) async-start(s8[8388608]{0:T(1024)(128)(4,1)} %bitcast.68), calls=%async_computation | async-start | bytes 8388608
  262.4 99.7 %slice-start.1 = ((s8[8388608]{0:T(1024)(128)(4,1)}), s8[4194304]{0:T(1024)(128)(4,1)S(1)}, s32[]{:S(2)}) async-start(s8[8388608]{0:T(1024)(128)(4,1)} %bitcast.68), calls=%async_computation.1 | async-start | bytes 8388608
  329.9 32.2 %copy-start.2 = (f32[256,1024]{1,0:T(8,128)}, f32[256,1024]{1,0:T(8,128)S(1)}, u32[]{:S(2)}) copy-start(f32[256,1024]{1,0:T(8,128)S(1)} %get-tuple-element.82) | copy-start | bytes 3145732
  362.2 4.0 copy-start.10
  422.1 1.0 copy-start.6
  427.0 2.0 copy-start.11
  448.6 2.1 copy-start.7
  450.7 1.2 copy-start.3

commit v2 on v1

--- a/solution.py
+++ b/solution.py
@@ -76,9 +76,9 @@
     relay = k == core
 
     def z_piece(i):
-        if i < blocks:
-            return xr.at[pl.ds(i * width, width)]
-        return gt.at[i - blocks]
+        if isinstance(i, int) and i >= blocks:
+            return gt.at[i - blocks]
+        return xr.at[pl.ds(i * width if isinstance(i, int) else pl.multiple_of(i * width, width), width)]
 
     def to_chip(i):
         return remote(z_piece(i), z_piece(i), send_z.at[i], recv_z.at[i], r, c + 2)
@@ -100,7 +100,7 @@
     step = half // RING_CHUNKS
 
     def ring_piece(side, i):
-        return xct.at[pl.ds(side * half + i * step, step)]
+        return xct.at[pl.ds(side * half + i * step if isinstance(i, int) else pl.multiple_of(side * half + i * step, step), step)]
 
     def to_after(i):
         return remote(ring_piece(0, i), ring_piece(0, i), send_a.at[i], recv_a.at[i], after, c)
@@ -144,17 +144,27 @@
 
         forward(blocks + 1)
 
-    for i in range(max(blocks + 2, RING_CHUNKS)):
-        if i < RING_CHUNKS:
-            @pl.when(ahead != 0)
-            def _(i=i):
-                to_after(i).wait_recv()
-                pl.when(ahead < rows - 1)(lambda: to_after(i).start())
-                to_before(i).wait_recv()
-                pl.when(behind < rows - 1)(lambda: to_before(i).start())
-        if i < blocks + 2:
-            @pl.when(jnp.logical_not(owner))
-            def _(i=i):
+    for t in range(max(blocks + 2 + chips - 1, RING_CHUNKS + rows - 2)):
+        i_after, i_before, i_z = t + 1 - ahead, t + 1 - behind, t - z
+
+        @pl.when((ahead != 0) & (i_after >= 0) & (i_after < RING_CHUNKS))
+        def _(i=i_after):
+            to_after(i).wait_recv()
+            pl.when(ahead < rows - 1)(lambda: to_after(i).start())
+
+        @pl.when((ahead != 0) & (i_before >= 0) & (i_before < RING_CHUNKS))
+        def _(i=i_before):
+            to_before(i).wait_recv()
+            pl.when(behind < rows - 1)(lambda: to_before(i).start())
+
+        @pl.when(jnp.logical_not(owner) & (i_z >= 0) & (i_z < blocks))
+        def _(i=i_z):
+            to_core(i).wait_recv()
+            pl.when(relay)(lambda: forward(i))
+
+        for extra in (blocks, blocks + 1):
+            @pl.when(jnp.logical_not(owner) & (i_z == extra))
+            def _(i=extra):
                 to_core(i).wait_recv()
                 pl.when(relay)(lambda: forward(i))
 

time: 489 us -> 400 us (0.82)
  Pallas kernels: 371 us -> 282 us
    pallas_call x2, Pallas kernels: 174 us -> 125 us  [reduce_product(): pl.pallas_call(functools.partial(product_kernel, rows, cols), out_shape=(...]
    pallas_call x2, Pallas kernels: 101 us -> 62.1 us  [spread(): pl.pallas_call(functools.partial(spread_kernel, panel, rows, cols), out_s...]
where the time goes in v2:
time: 400 us; the launch traced here: 394 us
  Pallas kernels  282 us (70%)
  matrix products  62.3 us (16%)
  local copies, waits for them, and re-layouts  32.2 us (8%)
  other arithmetic  16.7 us (4%)
    pallas_call x2, Pallas kernels, reduce_product(): pl.pallas_call(functools.partial(product_kernel, rows, cols), out_shape=(...  125 us
    pallas_call x2, Pallas kernels, spread(): pl.pallas_call(functools.partial(spread_kernel, panel, rows, cols), out_s...  62.1 us
    pallas_call x2, Pallas kernels, factors(): pl.pallas_call(factor_kernel, out_shape=(square,) * 3, in_specs=[VMEM], o...  60.1 us
    pallas_call x2, Pallas kernels, sum_rows(): pl.pallas_call(functools.partial(sum_kernel, rows), out_shape=jax.ShapeDt...  35 us
    dot_general x10, matrix products, dot(): jnp.dot(left, right, precision=precision, preferred_element_type=jnp.floa...  32.4 us
    dot_general x6, matrix products, dot_tn(): lax.dot_general(left, right, (((0,), (0,)), ((), ())), precision=highest,...  12.8 us
    unnamed x36, local copies, waits for them, and re-layouts  11.8 us
    reshape x1, local copies, waits for them, and re-layouts, shards(): return dense.reshape(matrix.shape)  10.5 us

profile of v2, /device:TPU:0, one launch (start us, length us, event | category | flops | bytes accessed | tf_op | source)
XLA Modules:
  0.0 394.4 jit_solution(8187416287735532876)
XLA Ops:
  0.0 8.9 %copy.8 = f32[256,8,4,256]{3,1,2,0:T(8,128)} copy(f32[256,8,4,256]{3,2,1,0:T(4,128)} %bitcast.79) | data formatting | bytes 16777216
  8.9 1.8 slice_select_fusion.1.xr_in
  10.7 1.4 slice.100
  12.1 0.2 copy.9
  12.3 0.0 slice-start.2
  12.3 0.1 broadcast_select_fusion.1.xct_in
  12.4 3.5 fusion.52.gram_in
  15.9 0.0 slice-start.3
  16.0 33.8 %spread_panel_0.1 = (f32[2048,256]{1,0:T(8,128)S(1)}, f32[256,1024]{1,0:T(8,128)S(1)}, f32[2,256,256]{2,1,0:T(8,128)S(1)}) custom-call(f32[2048,256]{1,0:T(8,128)S(1)} %slice_select_fusion.1.xr_in, f32[256,1024]{1,0:T(8,128)S(1)} %broadcast_select_fusion.1.xct_in, f32[256,256]{1,0:T(8,128)S(1)} %fusion.52.gram_in, f32[256,256]{1,0:T(8,128)S(1)} %slice.110.top_in), custom_call_target="tpu_custom_call" | custom-call | tf_op jit(solution)/shard_map/spread_panel_0/pallas_call | solution.py:192
  49.8 30.1 %factors_0.1 = (f32[256,256]{1,0:T(8,128)S(1)}, f32[256,256]{1,0:T(8,128)S(1)}, f32[256,256]{1,0:T(8,128)S(1)}) custom-call(f32[2,256,256]{2,1,0:T(8,128)S(1)} %get-tuple-element.70.gt), custom_call_target="tpu_custom_call" | custom-call | tf_op jit(solution)/shard_map/factors_0/pallas_call | solution.py:269
  79.8 2.1 convolution_add_fusion.1
  82.0 0.0 copy-done
  82.0 0.0 slice-done.2
  82.0 0.0 slice-done.3
  82.0 4.0 %convolution_select_fusion.1.part = f32[256,1024]{1,0:T(8,128)S(1)} fusion(f32[2048,256]{0,1:T(8,128)S(1)} %convolution_add_fusion.1, f32[2048,1024]{1,0:T(8,128)S(1)} %bitcast.74, pred[1024]{0:T(1024)(128)(4,1)S(1)} %get-tuple-element.102), kind=kOutput, calls=%fused_computation.41 | convolution fusion | flops 3221487616 | bytes 11535360 | tf_op jit(solution)/shard_map/dot_general | solution.py:449
  86.0 64.5 %reduce_product_0.1 = (f32[256,1024]{1,0:T(8,128)S(1)}, f32[2,256,1024]{2,1,0:T(8,128)S(1)}) custom-call(f32[256,1024]{1,0:T(8,128)S(1)} %convolution_select_fusion.1.part), custom_call_target="tpu_custom_call" | custom-call | tf_op jit(solution)/shard_map/reduce_product_0/pallas_call | solution.py:369
  150.6 1.0 copy-done.4
  151.6 2.0 reshape.223
  153.5 1.9 copy.4
  155.5 2.0 fusion.53
  157.5 1.9 fusion.54.part
  159.4 18.1 %sum_inner_0.1 = f32[256,256]{1,0:T(8,128)S(1)} custom-call(f32[256,256]{1,0:T(8,128)S(1)} %fusion.54.part), custom_call_target="tpu_custom_call" | custom-call | tf_op jit(solution)/shard_map/sum_inner_0/pallas_call | solution.py:409
  177.5 0.4 fusion.55
  177.9 0.4 fusion.56
  178.3 2.1 fusion.15
  180.5 1.0 fusion.57
  181.5 0.2 copy-done.1
  181.7 1.1 convolution_add_fusion.3
  182.8 1.0 fusion.25
  183.8 11.7 %fusion.11 = f32[2048,1024]{1,0:T(8,128)} fusion(f32[2048,1024]{1,0:T(8,128)} %bitcast.71, f32[2048,256]{0,1:T(8,128)S(1)} %copy-done.9, f32[2048,256]{0,1:T(8,128)S(1)} %fusion.15, f32[256,1024]{1,0:T(8,128)S(1)} %fusion.25, f32[256,1024]{1,0:T(8,128)S(1)} %convolution_add_fusion.3), kind=kOutput, calls=%fused_computation.9 | convolution fusion | flops 6446120960 | bytes 23068672 | tf_op jit(solution)/shard_map/dot_general | solution.py:18
  195.6 0.7 compare_reduce_fusion
  196.3 3.5 fusion.16
  199.8 0.1 copy.5
  200.0 0.2 tile.18
  200.2 0.2 copy.10
  200.4 2.5 broadcast_select_fusion
  202.9 1.9 slice_select_fusion.xr_in
  204.8 3.5 fusion.58.gram_in
  208.3 0.0 slice-start.1
  208.4 28.3 %spread_panel_1.1 = (f32[2048,256]{1,0:T(8,128)S(1)}, f32[256,1024]{1,0:T(8,128)S(1)}, f32[2,256,256]{2,1,0:T(8,128)S(1)}) custom-call(f32[2048,256]{1,0:T(8,128)S(1)} %slice_select_fusion.xr_in, f32[256,1024]{1,0:T(8,128)S(1)} %get-tuple-element.85.xct_in, f32[256,256]{1,0:T(8,128)S(1)} %fusion.58.gram_in, f32[256,256]{1,0:T(8,128)S(1)} %slice.114.top_in), custom_call_target="tpu_custom_call" | custom-call | tf_op jit(solution)/shard_map/spread_panel_1/pallas_call | solution.py:192
  236.7 30.1 %factors_1.1 = (f32[256,256]{1,0:T(8,128)S(1)}, f32[256,256]{1,0:T(8,128)S(1)}, f32[256,256]{1,0:T(8,128)S(1)}) custom-call(f32[2,256,256]{2,1,0:T(8,128)S(1)} %get-tuple-element.78.gt), custom_call_target="tpu_custom_call" | custom-call | tf_op jit(solution)/shard_map/factors_1/pallas_call | solution.py:269
  266.8 2.1 convolution_add_fusion
  269.0 4.0 %convolution_select_fusion.part = f32[256,1024]{1,0:T(8,128)S(1)} fusion(f32[2048,256]{0,1:T(8,128)S(1)} %convolution_add_fusion, f32[2048,1024]{1,0:T(8,128)S(1)} %bitcast.69, pred[1024]{0:T(1024)(128)(4,1)S(1)} %get-tuple-element.101), kind=kOutput, calls=%fused_computation.40 | convolution fusion | flops 3221487616 | bytes 11535360 | tf_op jit(solution)/shard_map/dot_general | solution.py:449
  273.0 60.6 %reduce_product_1.1 = (f32[256,1024]{1,0:T(8,128)S(1)}, f32[2,256,1024]{2,1,0:T(8,128)S(1)}) custom-call(f32[256,1024]{1,0:T(8,128)S(1)} %convolution_select_fusion.part), custom_call_target="tpu_custom_call" | custom-call | tf_op jit(solution)/shard_map/reduce_product_1/pallas_call | solution.py:369
  333.6 1.0 copy-done.6
  334.6 2.0 reshape.225
  336.5 1.9 copy.6
  338.5 2.0 fusion.59
  340.5 1.9 fusion.60.part
  342.4 16.9 %sum_inner_1.1 = f32[256,256]{1,0:T(8,128)S(1)} custom-call(f32[256,256]{1,0:T(8,128)S(1)} %fusion.60.part), custom_call_target="tpu_custom_call" | custom-call | tf_op jit(solution)/shard_map/sum_inner_1/pallas_call | solution.py:409
  359.3 0.4 fusion.61
  359.7 0.4 fusion.62
  360.1 2.1 fusion.14
  362.2 1.0 fusion.63
  363.3 0.2 copy-done.3
  363.4 1.1 convolution_add_fusion.2
  364.5 1.0 fusion.24
  365.6 11.5 %fusion.8 = f32[2048,1024]{1,0:T(8,128)} fusion(f32[2048,1024]{1,0:T(8,128)} %get-tuple-element.86, f32[2048,256]{0,1:T(8,128)S(1)} %copy-done.11, f32[2048,256]{0,1:T(8,128)S(1)} %fusion.14, f32[256,1024]{1,0:T(8,128)S(1)} %fusion.24, f32[256,1024]{1,0:T(8,128)S(1)} %convolution_add_fusion.2), kind=kOutput, calls=%fused_computation.8 | convolution fusion | flops 6446120960 | bytes 23068672 | tf_op jit(solution)/shard_map/dot_general | solution.py:18
  377.1 3.6 fusion.17
  380.8 0.1 copy.7
  380.9 0.2 tile.42
  381.1 0.2 copy.11
  381.3 2.4 fusion.26
  383.7 10.5 %reshape.227 = f32[8,256,4,256]{3,2,1,0:T(4,128)} reshape(f32[2048,1024]{1,0:T(8,128)} %fusion.26) | data formatting | bytes 16777216 | tf_op jit(solution)/shard_map/reshape | solution.py:473
  (34 shorter events, 0.2 us)
Async XLA Ops:
  12.3 69.7 %slice-start.2 = ((s8[8388608]{0:T(1024)(128)(4,1)}), s8[4194304]{0:T(1024)(128)(4,1)S(1)}, s32[]{:S(2)}) async-start(s8[8388608]{0:T(1024)(128)(4,1)} %bitcast.72), calls=%async_computation.2 | async-start | bytes 8388608
  15.9 66.1 %slice-start.3 = ((s8[8388608]{0:T(1024)(128)(4,1)}), s8[4194304]{0:T(1024)(128)(4,1)S(1)}, s32[]{:S(2)}) async-start(s8[8388608]{0:T(1024)(128)(4,1)} %bitcast.72), calls=%async_computation.3 | async-start | bytes 8388608
  49.8 32.2 %copy-start = (f32[256,1024]{1,0:T(8,128)}, f32[256,1024]{1,0:T(8,128)S(1)}, u32[]{:S(2)}) copy-start(f32[256,1024]{1,0:T(8,128)S(1)} %get-tuple-element.74) | copy-start | bytes 3145732
  82.0 4.0 %copy-start.8 = (f32[2048,256]{0,1:T(8,128)}, f32[2048,256]{0,1:T(8,128)S(1)}, u32[]{:S(2)}) copy-start(f32[2048,256]{0,1:T(8,128)S(1)} %convolution_add_fusion.1) | copy-start | bytes 6291460
  150.6 1.0 copy-start.4
  155.5 2.0 copy-start.9
  178.3 2.1 copy-start.5
  180.5 1.2 copy-start.1
  202.9 66.0 %slice-start = ((s8[8388608]{0:T(1024)(128)(4,1)}), s8[4194304]{0:T(1024)(128)(4,1)S(1)}, s32[]{:S(2)}) async-start(s8[8388608]{0:T(1024)(128)(4,1)} %bitcast.68), calls=%async_computation | async-start | bytes 8388608
  208.3 60.6 %slice-start.1 = ((s8[8388608]{0:T(1024)(128)(4,1)}), s8[4194304]{0:T(1024)(128)(4,1)S(1)}, s32[]{:S(2)}) async-start(s8[8388608]{0:T(1024)(128)(4,1)} %bitcast.68), calls=%async_computation.1 | async-start | bytes 8388608
  236.7 32.2 %copy-start.2 = (f32[256,1024]{1,0:T(8,128)}, f32[256,1024]{1,0:T(8,128)S(1)}, u32[]{:S(2)}) copy-start(f32[256,1024]{1,0:T(8,128)S(1)} %get-tuple-element.82) | copy-start | bytes 3145732
  269.0 4.0 %copy-start.10 = (f32[2048,256]{0,1:T(8,128)}, f32[2048,256]{0,1:T(8,128)S(1)}, u32[]{:S(2)}) copy-start(f32[2048,256]{0,1:T(8,128)S(1)} %convolution_add_fusion) | copy-start | bytes 6291460
  333.6 1.0 copy-start.6
  338.5 2.0 copy-start.11
  360.1 2.1 copy-start.7
  362.2 1.2 copy-start.3

commit v3 on v2

--- a/solution.py
+++ b/solution.py
@@ -48,161 +48,6 @@
 
 def ring_place(row, rows):
     return row + (row // 2) * (5 - 2 * row) if rows == 4 else row
-
-
-RING_CHUNKS = 4
-
-
-def spread_kernel(panel, rows, cols, xr_in, xct_in, gram_in, top_in, xr, xct, gt, slots,
-                  send_z, send_k, recv_z, send_a, recv_a, send_b, recv_b,
-                  send_g, recv_g, send_t, recv_t):
-    width = gram_in.shape[0]
-    r, c = lax.axis_index("row"), lax.axis_index("col")
-    z, k, chips = c // 2, c % 2, cols // 2
-    root_row, root_col, top_row = panel % rows, panel % cols, (panel + 1) % rows
-    core = root_col % 2
-    assert root_col // 2 == 0
-    blocks = xr.shape[0] // width
-    place = ring_place(r, rows)
-    after = ring_place((place + 1) % rows, rows)
-    before = ring_place((place + rows - 1) % rows, rows)
-    ahead = (place - ring_place(root_row, rows) + rows) % rows
-    behind = (rows - ahead) % rows
-    peers = [(r + i) % rows for i in range(1, rows)]
-    greet([(True, peer, c) for peer in peers]
-          + [(True, r, c + 1 - 2 * k), (z > 0, r, c - 2), (z < chips - 1, r, c + 2)])
-
-    owner = c == root_col
-    relay = k == core
-
-    def z_piece(i):
-        if isinstance(i, int) and i >= blocks:
-            return gt.at[i - blocks]
-        return xr.at[pl.ds(i * width if isinstance(i, int) else pl.multiple_of(i * width, width), width)]
-
-    def to_chip(i):
-        return remote(z_piece(i), z_piece(i), send_z.at[i], recv_z.at[i], r, c + 2)
-
-    def to_core(i):
-        return remote(z_piece(i), z_piece(i), send_k.at[i], recv_z.at[i], r, c + 1 - 2 * k)
-
-    def forward(i):
-        pl.when(z < chips - 1)(lambda: to_chip(i).start())
-        to_core(i).start()
-
-    def gram_to(i, peer):
-        return remote(gram_in, slots.at[i - 1], send_g.at[i - 1], recv_g.at[i - 1], peer, c)
-
-    def top_to(i, peer):
-        return remote(gt.at[1], gt.at[1], send_t.at[i - 1], recv_t, peer, c)
-
-    half = width // 2
-    step = half // RING_CHUNKS
-
-    def ring_piece(side, i):
-        return xct.at[pl.ds(side * half + i * step if isinstance(i, int) else pl.multiple_of(side * half + i * step, step), step)]
-
-    def to_after(i):
-        return remote(ring_piece(0, i), ring_piece(0, i), send_a.at[i], recv_a.at[i], after, c)
-
-    def to_before(i):
-        return remote(ring_piece(1, i), ring_piece(1, i), send_b.at[i], recv_b.at[i], before, c)
-
-    @pl.when(owner)
-    def _():
-        for i, peer in enumerate(peers, 1):
-            gram_to(i, peer).start()
-
-        @pl.when(r == top_row)
-        def _():
-            gt[1] = top_in[...]
-            for i, peer in enumerate(peers, 1):
-                top_to(i, peer).start()
-
-    @pl.when(ahead == 0)
-    def _():
-        xct[...] = xct_in[...]
-        for i in range(RING_CHUNKS):
-            to_after(i).start()
-            to_before(i).start()
-
-    @pl.when(owner)
-    def _():
-        for i in range(blocks):
-            xr[pl.ds(i * width, width), :] = xr_in[pl.ds(i * width, width), :]
-            forward(i)
-        total = gram_in[...]
-        for i, peer in enumerate(peers, 1):
-            gram_to(i, peer).wait()
-            total = total + slots[i - 1]
-        gt[0] = total
-        forward(blocks)
-
-        @pl.when(r != top_row)
-        def _():
-            top_to(1, peers[0]).wait_recv()
-
-        forward(blocks + 1)
-
-    for t in range(max(blocks + 2 + chips - 1, RING_CHUNKS + rows - 2)):
-        i_after, i_before, i_z = t + 1 - ahead, t + 1 - behind, t - z
-
-        @pl.when((ahead != 0) & (i_after >= 0) & (i_after < RING_CHUNKS))
-        def _(i=i_after):
-            to_after(i).wait_recv()
-            pl.when(ahead < rows - 1)(lambda: to_after(i).start())
-
-        @pl.when((ahead != 0) & (i_before >= 0) & (i_before < RING_CHUNKS))
-        def _(i=i_before):
-            to_before(i).wait_recv()
-            pl.when(behind < rows - 1)(lambda: to_before(i).start())
-
-        @pl.when(jnp.logical_not(owner) & (i_z >= 0) & (i_z < blocks))
-        def _(i=i_z):
-            to_core(i).wait_recv()
-            pl.when(relay)(lambda: forward(i))
-
-        for extra in (blocks, blocks + 1):
-            @pl.when(jnp.logical_not(owner) & (i_z == extra))
-            def _(i=extra):
-                to_core(i).wait_recv()
-                pl.when(relay)(lambda: forward(i))
-
-    @pl.when(owner & (r == top_row))
-    def _():
-        for i, peer in enumerate(peers, 1):
-            top_to(i, peer).wait_send()
-
-    @pl.when(relay)
-    def _():
-        for i in range(blocks + 2):
-            pl.when(z < chips - 1)(lambda: to_chip(i).wait_send())
-            to_core(i).wait_send()
-
-    for i in range(RING_CHUNKS):
-        pl.when(ahead < rows - 1)(lambda: to_after(i).wait_send())
-        pl.when(behind < rows - 1)(lambda: to_before(i).wait_send())
-
-
-def spread(panel, rows, cols, xr, xct, gram, top):
-    width = gram.shape[0]
-    pieces = xr.shape[0] // width + 2
-    dma = pltpu.SemaphoreType.DMA
-    f32 = jnp.float32
-    return pl.pallas_call(
-        functools.partial(spread_kernel, panel, rows, cols),
-        out_shape=(jax.ShapeDtypeStruct(xr.shape, f32), jax.ShapeDtypeStruct(xct.shape, f32),
-                   jax.ShapeDtypeStruct((2, width, width), f32)),
-        in_specs=[VMEM] * 4,
-        out_specs=(VMEM,) * 3,
-        scratch_shapes=[pltpu.VMEM((rows - 1, width, width), f32),
-                        dma((pieces,)), dma((pieces,)), dma((pieces,)),
-                        dma((RING_CHUNKS,)), dma((RING_CHUNKS,)), dma((RING_CHUNKS,)), dma((RING_CHUNKS,)),
-                        dma((rows - 1,)), dma((rows - 1,)), dma((rows - 1,)), dma],
-        compiler_params=pltpu.CompilerParams(collective_id=panel, has_side_effects=True,
-                                             vmem_limit_bytes=40 * 2**20),
-        name=f"spread_panel_{panel}",
-    )(xr, xct, gram, top)
 
 
 GROUP = 4
@@ -233,9 +78,10 @@
     return jnp.where(row >= col, work[:, size:] * lax.rsqrt(diagonal), 0.0)
 
 
-def factorize(work, size):
+def factor_steps(work, size):
     width = work.shape[0]
-    for start in range(0, width, size):
+
+    def step(start):
         stop = start + size
         inverse = eliminate(work[start:stop, start:stop])
         strip = dot(inverse, work[start:stop, :])
@@ -243,41 +89,219 @@
         if stop < width:
             work[stop:, :] = work[stop:, :] - dot_tn(strip[:, stop:width], strip)
 
-
-def factor_kernel(gt, upper, lower_inverse, coupling, work):
-    width = upper.shape[0]
+    return [functools.partial(step, start) for start in range(0, width, size)]
+
+
+def identity(width):
     row = lax.broadcasted_iota(jnp.int32, (width, width), 0)
     col = lax.broadcasted_iota(jnp.int32, (width, width), 1)
-    eye = (row == col).astype(jnp.float32)
-    work[:, :width] = gt[0]
-    work[:, width:] = eye
-    factorize(work, 64)
-    upper[...] = jnp.where(row <= col, work[:, :width], 0.0)
-    inverse = work[:, width:]
-    lower_inverse[...] = inverse
-    shifted = eye + dot_nt(gt[1], inverse)
-    work[:, :width] = dot_tn(shifted, shifted)
-    work[:, width:] = eye
-    factorize(work, 64)
-    inverse = work[:, width:]
-    coupling[...] = dot_tn(inverse, dot_nt(inverse, shifted))
-
-
-def factors(panel, gt):
-    width = gt.shape[1]
-    square = jax.ShapeDtypeStruct((width, width), jnp.float32)
+    return (row == col).astype(jnp.float32), row <= col
+
+
+def cholesky_steps(gram, upper, lower_inverse, work):
+    width = upper.shape[0]
+
+    def begin():
+        work[:, :width] = gram[...]
+        work[:, width:] = identity(width)[0]
+
+    def end():
+        upper[...] = jnp.where(identity(width)[1], work[:, :width], 0.0)
+        lower_inverse[...] = work[:, width:]
+
+    return [begin] + factor_steps(work, 64) + [end]
+
+
+def coupling_steps(top, lower_inverse, coupling, shifted, work):
+    width = coupling.shape[0]
+
+    def begin():
+        eye = identity(width)[0]
+        shifted[...] = eye + dot_nt(top[...], lower_inverse[...])
+        work[:, :width] = dot_tn(shifted[...], shifted[...])
+        work[:, width:] = eye
+
+    def end():
+        inverse = work[:, width:]
+        coupling[...] = dot_tn(inverse, dot_nt(inverse, shifted[...]))
+
+    return [begin] + factor_steps(work, 64) + [end]
+
+
+RING_CHUNKS = 4
+LEAD = 2
+
+
+def spread_kernel(panel, rows, cols, xr_in, xct_in, gram_in, top_in, xr, xct, gt, upper, lower_inverse,
+                  slots, work,
+                  send_z, send_k, recv_z, send_a, recv_a, send_b, recv_b,
+                  send_g, recv_g, send_t, recv_t):
+    width = gram_in.shape[0]
+    r, c = lax.axis_index("row"), lax.axis_index("col")
+    z, k, chips = c // 2, c % 2, cols // 2
+    root_row, root_col, top_row = panel % rows, panel % cols, (panel + 1) % rows
+    core = root_col % 2
+    assert root_col // 2 == 0
+    blocks = xr.shape[0] // width
+    place = ring_place(r, rows)
+    after = ring_place((place + 1) % rows, rows)
+    before = ring_place((place + rows - 1) % rows, rows)
+    ahead = (place - ring_place(root_row, rows) + rows) % rows
+    behind = (rows - ahead) % rows
+    peers = [(r + i) % rows for i in range(1, rows)]
+    greet([(True, peer, c) for peer in peers]
+          + [(True, r, c + 1 - 2 * k), (z > 0, r, c - 2), (z < chips - 1, r, c + 2)])
+
+    owner = c == root_col
+    relay = k == core
+
+    def z_piece(i):
+        if isinstance(i, int):
+            if i in (LEAD, LEAD + 1):
+                return gt.at[i - LEAD]
+            return xr.at[pl.ds((i if i < LEAD else i - 2) * width, width)]
+        place = i - 2 * (i > LEAD).astype(jnp.int32)
+        return xr.at[pl.ds(pl.multiple_of(place * width, width), width)]
+
+    def to_chip(i):
+        return remote(z_piece(i), z_piece(i), send_z.at[i], recv_z.at[i], r, c + 2)
+
+    def to_core(i):
+        return remote(z_piece(i), z_piece(i), send_k.at[i], recv_z.at[i], r, c + 1 - 2 * k)
+
+    def forward(i):
+        pl.when(z < chips - 1)(lambda: to_chip(i).start())
+        to_core(i).start()
+
+    def gram_to(i, peer):
+        return remote(gram_in, slots.at[i - 1], send_g.at[i - 1], recv_g.at[i - 1], peer, c)
+
+    def top_to(i, peer):
+        return remote(gt.at[1], gt.at[1], send_t.at[i - 1], recv_t, peer, c)
+
+    half = width // 2
+    step = half // RING_CHUNKS
+
+    def ring_piece(side, i):
+        return xct.at[pl.ds(side * half + i * step if isinstance(i, int) else pl.multiple_of(side * half + i * step, step), step)]
+
+    def to_after(i):
+        return remote(ring_piece(0, i), ring_piece(0, i), send_a.at[i], recv_a.at[i], after, c)
+
+    def to_before(i):
+        return remote(ring_piece(1, i), ring_piece(1, i), send_b.at[i], recv_b.at[i], before, c)
+
+    @pl.when(owner)
+    def _():
+        for i, peer in enumerate(peers, 1):
+            gram_to(i, peer).start()
+
+        @pl.when(r == top_row)
+        def _():
+            gt[1] = top_in[...]
+            for i, peer in enumerate(peers, 1):
+                top_to(i, peer).start()
+
+    @pl.when(ahead == 0)
+    def _():
+        xct[...] = xct_in[...]
+        for i in range(RING_CHUNKS):
+            to_after(i).start()
+            to_before(i).start()
+
+    @pl.when(owner)
+    def _():
+        for i in range(LEAD):
+            xr[pl.ds(i * width, width), :] = xr_in[pl.ds(i * width, width), :]
+            forward(i)
+        total = gram_in[...]
+        for i, peer in enumerate(peers, 1):
+            gram_to(i, peer).wait()
+            total = total + slots[i - 1]
+        gt[0] = total
+        forward(LEAD)
+
+        @pl.when(r != top_row)
+        def _():
+            top_to(1, peers[0]).wait_recv()
+
+        forward(LEAD + 1)
+        for i in range(LEAD, blocks):
+            xr[pl.ds(i * width, width), :] = xr_in[pl.ds(i * width, width), :]
+            forward(i + 2)
+
+    steps = cholesky_steps(gt.at[0], upper, lower_inverse, work)
+    for t in range(max(blocks + 2 + chips - 1, RING_CHUNKS + rows - 2)):
+        i_after, i_before, i_z = t + 1 - ahead, t + 1 - behind, t - z
+
+        @pl.when((ahead != 0) & (i_after >= 0) & (i_after < RING_CHUNKS))
+        def _(i=i_after):
+            to_after(i).wait_recv()
+            pl.when(ahead < rows - 1)(lambda: to_after(i).start())
+
+        @pl.when((ahead != 0) & (i_before >= 0) & (i_before < RING_CHUNKS))
+        def _(i=i_before):
+            to_before(i).wait_recv()
+            pl.when(behind < rows - 1)(lambda: to_before(i).start())
+
+        body = (i_z >= 0) & (i_z < blocks + 2) & ((i_z < LEAD) | (i_z > LEAD + 1))
+
+        @pl.when(jnp.logical_not(owner) & body)
+        def _(i=i_z):
+            to_core(i).wait_recv()
+            pl.when(relay)(lambda: forward(i))
+
+        for extra in (LEAD, LEAD + 1):
+            @pl.when(jnp.logical_not(owner) & (i_z == extra))
+            def _(i=extra):
+                to_core(i).wait_recv()
+                pl.when(relay)(lambda: forward(i))
+
+        if steps and t >= LEAD + chips:
+            steps.pop(0)()
+
+    for step_left in steps:
+        step_left()
+
+    @pl.when(owner & (r == top_row))
+    def _():
+        for i, peer in enumerate(peers, 1):
+            top_to(i, peer).wait_send()
+
+    @pl.when(relay)
+    def _():
+        for i in range(blocks + 2):
+            pl.when(z < chips - 1)(lambda: to_chip(i).wait_send())
+            to_core(i).wait_send()
+
+    for i in range(RING_CHUNKS):
+        pl.when(ahead < rows - 1)(lambda: to_after(i).wait_send())
+        pl.when(behind < rows - 1)(lambda: to_before(i).wait_send())
+
+
+def spread(panel, rows, cols, xr, xct, gram, top):
+    width = gram.shape[0]
+    pieces = xr.shape[0] // width + 2
+    dma = pltpu.SemaphoreType.DMA
+    f32 = jnp.float32
     return pl.pallas_call(
-        factor_kernel,
-        out_shape=(square,) * 3,
-        in_specs=[VMEM],
-        out_specs=(VMEM,) * 3,
-        scratch_shapes=[pltpu.VMEM((width, 2 * width), jnp.float32)],
-        compiler_params=pltpu.CompilerParams(vmem_limit_bytes=32 * 2**20),
-        name=f"factors_{panel}",
-    )(gt)
-
-
-def product_kernel(rows, cols, part, wct, wrt, slots, send_s, recv_s, send_g, recv_g,
+        functools.partial(spread_kernel, panel, rows, cols),
+        out_shape=(jax.ShapeDtypeStruct(xr.shape, f32), jax.ShapeDtypeStruct(xct.shape, f32),
+                   jax.ShapeDtypeStruct((2, width, width), f32),
+                   jax.ShapeDtypeStruct((width, width), f32), jax.ShapeDtypeStruct((width, width), f32)),
+        in_specs=[VMEM] * 4,
+        out_specs=(VMEM,) * 5,
+        scratch_shapes=[pltpu.VMEM((rows - 1, width, width), f32), pltpu.VMEM((width, 2 * width), f32),
+                        dma((pieces,)), dma((pieces,)), dma((pieces,)),
+                        dma((RING_CHUNKS,)), dma((RING_CHUNKS,)), dma((RING_CHUNKS,)), dma((RING_CHUNKS,)),
+                        dma((rows - 1,)), dma((rows - 1,)), dma((rows - 1,)), dma],
+        compiler_params=pltpu.CompilerParams(collective_id=panel, has_side_effects=True,
+                                             vmem_limit_bytes=40 * 2**20),
+        name=f"spread_panel_{panel}",
+    )(xr, xct, gram, top)
+
+
+def product_kernel(rows, cols, part, top, lower_inverse, wct, wrt, coupling, slots, work, shifted, send_s, recv_s, send_g, recv_g,
                    send_up, send_down, send_k, recv_z):
     r, c = lax.axis_index("row"), lax.axis_index("col")
     z, k, chips = c // 2, c % 2, cols // 2
@@ -301,6 +325,9 @@
 
     for i in range(1, rows):
         scatter(i).start()
+    steps = coupling_steps(top, lower_inverse, coupling, shifted, work)
+    steps.pop(0)()
+    steps.pop(0)()
     total = part[rows_of(r), :]
     for i in range(1, rows):
         scatter(i).wait_recv()
@@ -308,6 +335,7 @@
     wct[rows_of(r), :] = total
     for i in range(1, rows):
         gather(i).start()
+    steps.pop(0)()
 
     def origin(h):
         return (r + rows * h) // 2
@@ -347,6 +375,11 @@
                     pl.when((z > origin(h)) & (z < chips - 1))(lambda: up(h, i).start())
                     pl.when((z < origin(h)) & (z > 0))(lambda: down(h, i).start())
                     across(h, i).start()
+        if steps:
+            steps.pop(0)()
+
+    for step_left in steps:
+        step_left()
 
     for i in range(1, rows):
         scatter(i).wait_send()
@@ -361,7 +394,7 @@
                 across(h, i).wait_send()
 
 
-def reduce_product(panel, rows, cols, part):
+def reduce_product(panel, rows, cols, part, top, lower_inverse):
     width, local_cols = part.shape
     halves = cols // rows
     dma = pltpu.SemaphoreType.DMA
@@ -369,16 +402,18 @@
     return pl.pallas_call(
         functools.partial(product_kernel, rows, cols),
         out_shape=(jax.ShapeDtypeStruct(part.shape, f32),
-                   jax.ShapeDtypeStruct((halves, width, local_cols), f32)),
-        in_specs=[VMEM],
-        out_specs=(VMEM,) * 2,
+                   jax.ShapeDtypeStruct((halves, width, local_cols), f32),
+                   jax.ShapeDtypeStruct((width, width), f32)),
+        in_specs=[VMEM] * 3,
+        out_specs=(VMEM,) * 3,
         scratch_shapes=[pltpu.VMEM((rows - 1, width // rows, local_cols), f32),
+                        pltpu.VMEM((width, 2 * width), f32), pltpu.VMEM((width, width), f32),
                         dma((rows - 1,)), dma((rows - 1,)), dma((rows - 1,)), dma((rows - 1,)),
                         dma((halves, rows)), dma((halves, rows)), dma((halves, rows)), dma((halves, rows))],
         compiler_params=pltpu.CompilerParams(collective_id=PANELS + panel, has_side_effects=True,
                                              vmem_limit_bytes=40 * 2**20),
         name=f"reduce_product_{panel}",
-    )(part)
+    )(part, top, lower_inverse)
 
 
 def sum_kernel(rows, part, out, slots, send_s, recv_s, send_k, recv_k):
@@ -439,9 +474,8 @@
         low = jnp.where(below, dense[:, col_slot:col_slot + width], 0.0)
         right = jnp.where(beside, dense[row_slot:row_slot + width, :], 0.0)
         top_slot = (panel + 1) // rows * width
-        xr, xct, gt = spread(panel, rows, cols, low, right, dot_tn(low, low),
-                             low[top_slot:top_slot + width])
-        upper, lower_inverse, coupling = factors(panel, gt)
+        xr, xct, gt, upper, lower_inverse = spread(panel, rows, cols, low, right, dot_tn(low, low),
+                                                   low[top_slot:top_slot + width])
         placed_rows = (global_rows[:, None] - start == unit[None, :]).astype(jnp.float32)
         placed_cols = (global_cols[None, :] - start == unit[:, None]).astype(jnp.float32)
         vec_rows = dot_nt(xr, lower_inverse) + placed_rows
@@ -449,7 +483,7 @@
         part = lax.dot_general(vec_rows, dense, (((0,), (0,)), ((), ())), precision=high,
                                preferred_element_type=jnp.float32)
         part = jnp.where(beside, part, 0.0)
-        applied_cols, applied = reduce_product(panel, rows, cols, part)
+        applied_cols, applied, coupling = reduce_product(panel, rows, cols, part, gt[1], lower_inverse)
         applied = applied.reshape(halves, width, col_blocks, width)
         applied_rows = applied.transpose(2, 0, 3, 1).reshape(local_rows, width)
         inner = sum_rows(panel, rows, dot_tn(vec_rows, applied_rows))

time: 400 us -> 350 us (0.88)
  Pallas kernels: 282 us -> 231 us
    pallas_call x2 -> x0, Pallas kernels: 60.1 us -> none  [factors(): pl.pallas_call(factor_kernel, out_shape=(square,) * 3, in_specs=[VMEM], o...]
    pallas_call x2, Pallas kernels: 62.1 us -> 83.3 us  [spread(): pl.pallas_call(functools.partial(spread_kernel, panel, rows, cols), out_s...]
    pallas_call x2, Pallas kernels: 125 us -> 112 us  [reduce_product(): pl.pallas_call(functools.partial(product_kernel, rows, cols), out_shape=(...]
where the time goes in v3:
time: 350 us; the launch traced here: 344 us
  Pallas kernels  231 us (66%)
  matrix products  62.7 us (18%)
  local copies, waits for them, and re-layouts  32.8 us (9%)
  other arithmetic  16.5 us (5%)
    pallas_call x2, Pallas kernels, reduce_product(): pl.pallas_call(functools.partial(product_kernel, rows, cols), out_shape=(...  112 us
    pallas_call x2, Pallas kernels, spread(): pl.pallas_call(functools.partial(spread_kernel, panel, rows, cols), out_s...  83.3 us
    pallas_call x2, Pallas kernels, sum_rows(): pl.pallas_call(functools.partial(sum_kernel, rows), out_shape=jax.ShapeDt...  35.3 us
    dot_general x10, matrix products, dot(): jnp.dot(left, right, precision=precision, preferred_element_type=jnp.floa...  32.4 us
    dot_general x6, matrix products, dot_tn(): lax.dot_general(left, right, (((0,), (0,)), ((), ())), precision=highest,...  12.8 us
    unnamed x36, local copies, waits for them, and re-layouts  11.8 us
    reshape x1, local copies, waits for them, and re-layouts, shards(): return dense.reshape(matrix.shape)  10.5 us
    dot_general x6, matrix products, dot_nt(): lax.dot_general(left, right, (((1,), (1,)), ((), ())), precision=highest,...  9.11 us

profile of v3, /device:TPU:0, one launch (start us, length us, event | category | flops | bytes accessed | tf_op | source)
XLA Modules:
  0.0 343.9 jit_solution(6136493582688454451)
XLA Ops:
  0.0 8.9 %copy.8 = f32[256,8,4,256]{3,1,2,0:T(8,128)} copy(f32[256,8,4,256]{3,2,1,0:T(4,128)} %bitcast.83) | data formatting | bytes 16777216
  8.9 1.8 slice_select_fusion.1.xr_in
  10.7 1.4 slice.106
  12.1 0.2 copy.9
  12.3 0.0 slice-start.2
  12.3 0.1 broadcast_select_fusion.1.xct_in
  12.4 3.5 %fusion.52.gram_in = f32[256,256]{1,0:T(8,128)S(1)} fusion(f32[2048,256]{1,0:T(8,128)S(1)} %slice_select_fusion.1.xr_in), kind=kOutput, calls=%fused_computation.97 | convolution fusion | flops 1610612736 | bytes 2359296 | tf_op jit(solution)/shard_map/dot_general | solution.py:22
  15.9 0.0 slice-start.3
  16.0 40.4 %spread_panel_0.1 = (f32[2048,256]{1,0:T(8,128)S(1)}, f32[256,1024]{1,0:T(8,128)S(1)}, f32[2,256,256]{2,1,0:T(8,128)S(1)}, f32[256,256]{1,0:T(8,128)S(1)}, f32[256,256]{1,0:T(8,128)S(1)}) custom-call(f32[2048,256]{1,0:T(8,128)S(1)} %slice_select_fusion.1.xr_in, f32[256,1024]{1,0:T(8,128)S(1)} %broadcast_select_fusion.1.xct_in, ...), custom_call_target="tpu_custom_call" | custom-call | tf_op jit(solution)/shard_map/spread_panel_0/pallas_call | solution.py:287
  56.4 2.1 convolution_add_fusion.1
  58.6 4.2 %convolution_select_fusion.1.part = f32[256,1024]{1,0:T(8,128)S(1)} fusion(f32[2048,256]{0,1:T(8,128)S(1)} %convolution_add_fusion.1, f32[2048,1024]{1,0:T(8,128)S(1)} %bitcast.78, pred[1024]{0:T(1024)(128)(4,1)S(1)} %get-tuple-element.102), kind=kOutput, calls=%fused_computation.41 | convolution fusion | flops 3221487616 | bytes 11535360 | tf_op jit(solution)/shard_map/dot_general | solution.py:483
  62.7 0.0 copy-done.8
  62.8 62.0 %reduce_product_0.1 = (f32[256,1024]{1,0:T(8,128)S(1)}, f32[2,256,1024]{2,1,0:T(8,128)S(1)}, f32[256,256]{1,0:T(8,128)S(1)}) custom-call(f32[256,1024]{1,0:T(8,128)S(1)} %convolution_select_fusion.1.part, f32[256,256]{1,0:T(8,128)S(1)} %slice_bitcast_fusion.1.top, f32[256,256]{1,0:T(8,128)S(1)} %get-tuple-element.70.lower_inverse), custom_call_target="tpu_custom_call" | custom-call | tf_op jit(solution)/shard_map/reduce_product_0/pallas_call | solution.py:402
  124.8 1.0 copy-done.4
  125.8 2.2 reshape.223
  128.0 1.9 copy.4
  129.9 2.0 fusion.53
  131.9 0.0 copy-done.9
  131.9 1.9 fusion.54.part
  133.8 17.8 %sum_inner_0.1 = f32[256,256]{1,0:T(8,128)S(1)} custom-call(f32[256,256]{1,0:T(8,128)S(1)} %fusion.54.part), custom_call_target="tpu_custom_call" | custom-call | tf_op jit(solution)/shard_map/sum_inner_0/pallas_call | solution.py:444
  151.6 0.4 fusion.55
  152.0 0.4 fusion.56
  152.4 2.1 fusion.15
  154.6 1.0 fusion.57
  155.6 0.2 copy-done.1
  155.8 1.1 convolution_add_fusion.3
  156.9 1.0 fusion.25
  157.9 11.7 %fusion.11 = f32[2048,1024]{1,0:T(8,128)} fusion(f32[2048,1024]{1,0:T(8,128)} %bitcast.75, f32[2048,256]{0,1:T(8,128)S(1)} %copy-done.9, f32[2048,256]{0,1:T(8,128)S(1)} %fusion.15, f32[256,1024]{1,0:T(8,128)S(1)} %fusion.25, f32[256,1024]{1,0:T(8,128)S(1)} %convolution_add_fusion.3), kind=kOutput, calls=%fused_computation.9 | convolution fusion | flops 6446120960 | bytes 23068672 | tf_op jit(solution)/shard_map/dot_general | solution.py:18
  169.6 0.6 compare_reduce_fusion
  170.3 3.4 %fusion.16 = f32[2048,1024]{1,0:T(8,128)} fusion(f32[2048,1024]{1,0:T(8,128)} %fusion.11, pred[2048]{0:T(1024)(128)(4,1)S(1)} %get-tuple-element.96, pred[]{:T(512)S(6)} %eq.74, pred[]{:T(512)} %compare_reduce_fusion, f32[256,256]{1,0:T(8,128)S(1)} %get-tuple-element.90, pred[2048]{0:T(1024)(128)(4,1)S(1)} %get-tuple-element.92), kind=kLoop, calls=%fused_computation.18 | loop fusion | flops 2097152 | bytes 4461057 | tf_op jit(solution)/shard_map/scatter | solution.py:499
  173.8 0.1 copy.5
  173.9 0.2 tile.18
  174.1 0.2 copy.10
  174.3 2.5 broadcast_select_fusion
  176.8 1.9 slice_select_fusion.xr_in
  178.8 3.5 %fusion.58.gram_in = f32[256,256]{1,0:T(8,128)S(1)} fusion(f32[2048,256]{1,0:T(8,128)S(1)} %slice_select_fusion.xr_in), kind=kOutput, calls=%fused_computation.103 | convolution fusion | flops 1610612736 | bytes 2359296 | tf_op jit(solution)/shard_map/dot_general | solution.py:22
  182.3 0.0 slice-start.1
  182.3 42.9 %spread_panel_1.1 = (f32[2048,256]{1,0:T(8,128)S(1)}, f32[256,1024]{1,0:T(8,128)S(1)}, f32[2,256,256]{2,1,0:T(8,128)S(1)}, f32[256,256]{1,0:T(8,128)S(1)}, f32[256,256]{1,0:T(8,128)S(1)}) custom-call(f32[2048,256]{1,0:T(8,128)S(1)} %slice_select_fusion.xr_in, f32[256,1024]{1,0:T(8,128)S(1)} %get-tuple-element.85.xct_in, f32[256,256]{1,0:T(8,128)S(1)} %fusion.58.gram_in, ...), custom_call_target="tpu_custom_call" | custom-call | tf_op jit(solution)/shard_map/spread_panel_1/pallas_call | solution.py:287
  225.2 2.1 convolution_add_fusion
  227.3 0.0 copy-done.2
  227.4 0.0 slice-done
  227.4 0.0 slice-done.1
  227.4 4.2 %convolution_select_fusion.part = f32[256,1024]{1,0:T(8,128)S(1)} fusion(f32[2048,256]{0,1:T(8,128)S(1)} %convolution_add_fusion, f32[2048,1024]{1,0:T(8,128)S(1)} %bitcast.73, pred[1024]{0:T(1024)(128)(4,1)S(1)} %get-tuple-element.101), kind=kOutput, calls=%fused_computation.40 | convolution fusion | flops 3221487616 | bytes 11535360 | tf_op jit(solution)/shard_map/dot_general | solution.py:483
  231.7 50.4 %reduce_product_1.1 = (f32[256,1024]{1,0:T(8,128)S(1)}, f32[2,256,1024]{2,1,0:T(8,128)S(1)}, f32[256,256]{1,0:T(8,128)S(1)}) custom-call(f32[256,1024]{1,0:T(8,128)S(1)} %convolution_select_fusion.part, f32[256,256]{1,0:T(8,128)S(1)} %slice_bitcast_fusion.top, f32[256,256]{1,0:T(8,128)S(1)} %get-tuple-element.78.lower_inverse), custom_call_target="tpu_custom_call" | custom-call | tf_op jit(solution)/shard_map/reduce_product_1/pallas_call | solution.py:402
  282.1 1.0 copy-done.6
  283.1 2.4 reshape.225
  285.4 1.9 copy.6
  287.4 2.0 fusion.59
  289.4 1.9 fusion.60.part
  291.3 17.5 %sum_inner_1.1 = f32[256,256]{1,0:T(8,128)S(1)} custom-call(f32[256,256]{1,0:T(8,128)S(1)} %fusion.60.part), custom_call_target="tpu_custom_call" | custom-call | tf_op jit(solution)/shard_map/sum_inner_1/pallas_call | solution.py:444
  308.8 0.4 fusion.61
  309.2 0.4 fusion.62
  309.6 2.1 fusion.14
  311.8 1.0 fusion.63
  312.8 0.2 copy-done.3
  313.0 1.1 convolution_add_fusion.2
  314.1 1.0 fusion.24
  315.1 11.5 %fusion.8 = f32[2048,1024]{1,0:T(8,128)} fusion(f32[2048,1024]{1,0:T(8,128)} %get-tuple-element.86, f32[2048,256]{0,1:T(8,128)S(1)} %copy-done.11, f32[2048,256]{0,1:T(8,128)S(1)} %fusion.14, f32[256,1024]{1,0:T(8,128)S(1)} %fusion.24, f32[256,1024]{1,0:T(8,128)S(1)} %convolution_add_fusion.2), kind=kOutput, calls=%fused_computation.8 | convolution fusion | flops 6446120960 | bytes 23068672 | tf_op jit(solution)/shard_map/dot_general | solution.py:18
  326.6 3.6 %fusion.17 = f32[2048,1024]{1,0:T(8,128)} fusion(f32[2048,1024]{1,0:T(8,128)} %fusion.8, pred[2048]{0:T(1024)(128)(4,1)S(1)} %get-tuple-element.95, pred[]{:T(512)S(6)} %eq.82, pred[]{:T(512)} %compare_reduce_fusion, f32[256,256]{1,0:T(8,128)S(1)} %get-tuple-element.88, pred[2048]{0:T(1024)(128)(4,1)S(1)} %get-tuple-element.91), kind=kLoop, calls=%fused_computation.19 | loop fusion | flops 2097152 | bytes 4461057 | tf_op jit(solution)/shard_map/scatter | solution.py:499
  330.2 0.1 copy.7
  330.4 0.2 tile.42
  330.5 0.2 copy.11
  330.8 2.4 fusion.26
  333.2 10.5 %reshape.227 = f32[8,256,4,256]{3,2,1,0:T(4,128)} reshape(f32[2048,1024]{1,0:T(8,128)} %fusion.26) | data formatting | bytes 16777216 | tf_op jit(solution)/shard_map/reshape | solution.py:507
  (34 shorter events, 0.3 us)
Async XLA Ops:
  12.3 46.2 %slice-start.2 = ((s8[8388608]{0:T(1024)(128)(4,1)}), s8[4194304]{0:T(1024)(128)(4,1)S(1)}, s32[]{:S(2)}) async-start(s8[8388608]{0:T(1024)(128)(4,1)} %bitcast.76), calls=%async_computation.2 | async-start | bytes 8388608
  15.9 42.6 %slice-start.3 = ((s8[8388608]{0:T(1024)(128)(4,1)}), s8[4194304]{0:T(1024)(128)(4,1)S(1)}, s32[]{:S(2)}) async-start(s8[8388608]{0:T(1024)(128)(4,1)} %bitcast.76), calls=%async_computation.3 | async-start | bytes 8388608
  56.4 2.2 copy-start
  58.6 4.2 %copy-start.8 = (f32[2048,256]{0,1:T(8,128)}, f32[2048,256]{0,1:T(8,128)S(1)}, u32[]{:S(2)}) copy-start(f32[2048,256]{0,1:T(8,128)S(1)} %convolution_add_fusion.1) | copy-start | bytes 6291460
  124.8 1.0 copy-start.4
  129.9 2.0 copy-start.9
  152.4 2.1 copy-start.5
  154.5 1.2 copy-start.1
  176.8 50.5 %slice-start = ((s8[8388608]{0:T(1024)(128)(4,1)}), s8[4194304]{0:T(1024)(128)(4,1)S(1)}, s32[]{:S(2)}) async-start(s8[8388608]{0:T(1024)(128)(4,1)} %bitcast.72), calls=%async_computation | async-start | bytes 8388608
  182.3 45.1 %slice-start.1 = ((s8[8388608]{0:T(1024)(128)(4,1)}), s8[4194304]{0:T(1024)(128)(4,1)S(1)}, s32[]{:S(2)}) async-start(s8[8388608]{0:T(1024)(128)(4,1)} %bitcast.72), calls=%async_computation.1 | async-start | bytes 8388608
  225.2 2.2 copy-start.2
  227.4 4.2 %copy-start.10 = (f32[2048,256]{0,1:T(8,128)}, f32[2048,256]{0,1:T(8,128)S(1)}, u32[]{:S(2)}) copy-start(f32[2048,256]{0,1:T(8,128)S(1)} %convolution_add_fusion) | copy-start | bytes 6291460
  282.1 1.0 copy-start.6
  287.4 2.0 copy-start.11
  309.6 2.1 copy-start.7
  311.7 1.2 copy-start.3

commit v4 on v3

--- a/solution.py
+++ b/solution.py
@@ -301,7 +301,8 @@
     )(xr, xct, gram, top)
 
 
-def product_kernel(rows, cols, part, top, lower_inverse, wct, wrt, coupling, slots, work, shifted, send_s, recv_s, send_g, recv_g,
+def product_kernel(rows, cols, part, top, lower_inverse, vec_cols, wct, wrt, coupling, inner, slots, work, shifted,
+                   give, take, send_i, recv_i, send_j, recv_j, send_l, recv_l, send_s, recv_s, send_g, recv_g,
                    send_up, send_down, send_k, recv_z):
     r, c = lax.axis_index("row"), lax.axis_index("col")
     z, k, chips = c // 2, c % 2, cols // 2
@@ -309,8 +310,8 @@
     halves = cols // rows
     relay = k == r % 2
     peers = [(r + i) % rows for i in range(1, rows)]
-    greet([(True, peer, c) for peer in peers]
-          + [(True, r, c + 1 - 2 * k), (z > 0, r, c - 2), (z < chips - 1, r, c + 2)])
+    col_peers = [(c + i) % cols for i in range(1, cols)]
+    greet([(True, peer, c) for peer in peers] + [(True, r, peer) for peer in col_peers])
 
     def rows_of(q):
         return pl.ds(pl.multiple_of(q * share, share), share)
@@ -335,7 +336,42 @@
     wct[rows_of(r), :] = total
     for i in range(1, rows):
         gather(i).start()
+
+    size = share // cols
+    term = dot_nt(total, vec_cols[...])
+    for d in range(cols):
+        give[d] = term[d * size:(d + 1) * size, :]
+
+    def inner_scatter(i):
+        return remote(give.at[col_peers[i - 1]], take.at[i - 1], send_i.at[i - 1], recv_i.at[i - 1],
+                      r, col_peers[i - 1])
+
+    def inner_gather(i):
+        return remote(inner.at[r, c], inner.at[r, c], send_j.at[i - 1], recv_j.at[i - 1],
+                      r, col_peers[i - 1])
+
+    def inner_rows(i):
+        return remote(inner.at[r], inner.at[r], send_l.at[i - 1], recv_l.at[i - 1], peers[i - 1], c)
+
+    def inner_sum():
+        piece = give[c]
+        for i in range(1, cols):
+            inner_scatter(i).wait_recv()
+            piece = piece + take[i - 1]
+        inner[r, c] = piece
+        for i in range(1, cols):
+            inner_gather(i).start()
+
+    def inner_share():
+        for i in range(1, cols):
+            inner_gather(i).wait_recv()
+        for i in range(1, rows):
+            inner_rows(i).start()
+
+    for i in range(1, cols):
+        inner_scatter(i).start()
     steps.pop(0)()
+    rounds = [inner_sum, inner_share]
 
     def origin(h):
         return (r + rows * h) // 2
@@ -375,11 +411,19 @@
                     pl.when((z > origin(h)) & (z < chips - 1))(lambda: up(h, i).start())
                     pl.when((z < origin(h)) & (z > 0))(lambda: down(h, i).start())
                     across(h, i).start()
+        if rounds:
+            rounds.pop(0)()
         if steps:
             steps.pop(0)()
 
-    for step_left in steps:
+    for step_left in rounds + steps:
         step_left()
+
+    for i in range(1, cols):
+        inner_scatter(i).wait_send()
+        inner_gather(i).wait_send()
+    for i in range(1, rows):
+        inner_rows(i).wait()
 
     for i in range(1, rows):
         scatter(i).wait_send()
@@ -394,64 +438,30 @@
                 across(h, i).wait_send()
 
 
-def reduce_product(panel, rows, cols, part, top, lower_inverse):
+def reduce_product(panel, rows, cols, part, top, lower_inverse, vec_cols):
     width, local_cols = part.shape
-    halves = cols // rows
+    halves, size = cols // rows, width // (rows * cols)
     dma = pltpu.SemaphoreType.DMA
     f32 = jnp.float32
     return pl.pallas_call(
         functools.partial(product_kernel, rows, cols),
         out_shape=(jax.ShapeDtypeStruct(part.shape, f32),
                    jax.ShapeDtypeStruct((halves, width, local_cols), f32),
-                   jax.ShapeDtypeStruct((width, width), f32)),
-        in_specs=[VMEM] * 3,
-        out_specs=(VMEM,) * 3,
+                   jax.ShapeDtypeStruct((width, width), f32),
+                   jax.ShapeDtypeStruct((rows, cols, size, width), f32)),
+        in_specs=[VMEM] * 4,
+        out_specs=(VMEM,) * 4,
         scratch_shapes=[pltpu.VMEM((rows - 1, width // rows, local_cols), f32),
                         pltpu.VMEM((width, 2 * width), f32), pltpu.VMEM((width, width), f32),
+                        pltpu.VMEM((cols, size, width), f32), pltpu.VMEM((cols - 1, size, width), f32),
+                        dma((cols - 1,)), dma((cols - 1,)), dma((cols - 1,)), dma((cols - 1,)),
+                        dma((rows - 1,)), dma((rows - 1,)),
                         dma((rows - 1,)), dma((rows - 1,)), dma((rows - 1,)), dma((rows - 1,)),
                         dma((halves, rows)), dma((halves, rows)), dma((halves, rows)), dma((halves, rows))],
         compiler_params=pltpu.CompilerParams(collective_id=PANELS + panel, has_side_effects=True,
                                              vmem_limit_bytes=40 * 2**20),
         name=f"reduce_product_{panel}",
-    )(part, top, lower_inverse)
-
-
-def sum_kernel(rows, part, out, slots, send_s, recv_s, send_k, recv_k):
-    r, c = lax.axis_index("row"), lax.axis_index("col")
-    k = c % 2
-    half = part.shape[0] // 2
-    peers = [(r + i) % rows for i in range(1, rows)]
-    greet([(True, peer, c) for peer in peers] + [(True, r, c + 1 - 2 * k)])
-    mine = pl.ds(pl.multiple_of(k * half, half), half)
-
-    def send(i):
-        return remote(part.at[mine], slots.at[i - 1], send_s.at[i - 1], recv_s.at[i - 1], peers[i - 1], c)
-
-    for i in range(1, rows):
-        send(i).start()
-    total = part[mine, :]
-    for i in range(1, rows):
-        send(i).wait()
-        total = total + slots[i - 1]
-    out[mine, :] = total
-    swap = remote(out.at[mine], out.at[mine], send_k, recv_k, r, c + 1 - 2 * k)
-    swap.start()
-    swap.wait()
-
-
-def sum_rows(panel, rows, part):
-    dma = pltpu.SemaphoreType.DMA
-    return pl.pallas_call(
-        functools.partial(sum_kernel, rows),
-        out_shape=jax.ShapeDtypeStruct(part.shape, jnp.float32),
-        in_specs=[VMEM],
-        out_specs=VMEM,
-        scratch_shapes=[pltpu.VMEM((rows - 1, part.shape[0] // 2, part.shape[1]), jnp.float32),
-                        dma((rows - 1,)), dma((rows - 1,)), dma, dma],
-        compiler_params=pltpu.CompilerParams(collective_id=2 * PANELS + panel, has_side_effects=True,
-                                             vmem_limit_bytes=32 * 2**20),
-        name=f"sum_inner_{panel}",
-    )(part)
+    )(part, top, lower_inverse, vec_cols)
 
 
 def shards(matrix):
@@ -483,10 +493,11 @@
         part = lax.dot_general(vec_rows, dense, (((0,), (0,)), ((), ())), precision=high,
                                preferred_element_type=jnp.float32)
         part = jnp.where(beside, part, 0.0)
-        applied_cols, applied, coupling = reduce_product(panel, rows, cols, part, gt[1], lower_inverse)
+        applied_cols, applied, coupling, inner = reduce_product(panel, rows, cols, part, gt[1],
+                                                                lower_inverse, vec_cols)
+        inner = inner.reshape(width, width)
         applied = applied.reshape(halves, width, col_blocks, width)
         applied_rows = applied.transpose(2, 0, 3, 1).reshape(local_rows, width)
-        inner = sum_rows(panel, rows, dot_tn(vec_rows, applied_rows))
         middle = dot_nt(dot(coupling, inner), coupling)
         factor_rows = dot_nt(applied_rows, coupling) - 0.5 * dot(vec_rows, middle)
         factor_cols = dot(coupling, applied_cols) - 0.5 * dot_tn(middle, vec_cols)

time: 350 us -> 347 us (level)
  the two profiles are of different devices: /device:TPU:0 before, /device:TPU:5 now
where the time goes in v4:
time: 347 us; the launch traced here: 342 us
  Pallas kernels  236 us (68%)
  matrix products  54.3 us (16%)
  local copies, waits for them, and re-layouts  33.8 us (10%)
  other arithmetic  16.9 us (5%)
    pallas_call x2, Pallas kernels, reduce_product(): pl.pallas_call(functools.partial(product_kernel, rows, cols), out_shape=(...  154 us
    pallas_call x2, Pallas kernels, spread(): pl.pallas_call(functools.partial(spread_kernel, panel, rows, cols), out_s...  81.7 us
    dot_general x10, matrix products, dot(): jnp.dot(left, right, precision=precision, preferred_element_type=jnp.floa...  27.5 us
    unnamed x52, local copies, waits for them, and re-layouts  13 us
    reshape x1, local copies, waits for them, and re-layouts, shards(): return dense.reshape(matrix.shape)  10.5 us
    dot_general x6, matrix products, dot_nt(): lax.dot_general(left, right, (((1,), (1,)), ((), ())), precision=highest,...  9.14 us
    dot_general x4, matrix products, dot_tn(): lax.dot_general(left, right, (((0,), (0,)), ((), ())), precision=highest,...  9.06 us
    dot_general x2, matrix products, shards(): lax.dot_general(vec_rows, dense, (((0,), (0,)), ((), ())), precision=high...  8.62 us

profile of v4, /device:TPU:5, one launch (start us, length us, event | category | flops | bytes accessed | tf_op | source)
XLA Modules:
  0.0 341.5 jit_solution(7202843501638578354)
XLA Ops:
  0.0 8.9 %copy.8 = f32[256,8,4,256]{3,1,2,0:T(8,128)} copy(f32[256,8,4,256]{3,2,1,0:T(4,128)} %bitcast.83) | data formatting | bytes 16777216
  8.9 1.8 slice_select_fusion.1.xr_in
  10.7 1.4 slice.106
  12.1 0.2 copy.9
  12.3 0.0 slice-start.4
  12.3 0.1 broadcast_select_fusion.1.xct_in
  12.4 3.5 %fusion.52.gram_in = f32[256,256]{1,0:T(8,128)S(1)} fusion(f32[2048,256]{1,0:T(8,128)S(1)} %slice_select_fusion.1.xr_in), kind=kOutput, calls=%fused_computation.97 | convolution fusion | flops 1610612736 | bytes 2359296 | tf_op jit(solution)/shard_map/dot_general | solution.py:22
  15.9 0.0 slice-start.5
  16.0 39.2 %spread_panel_0.1 = (f32[2048,256]{1,0:T(8,128)S(1)}, f32[256,1024]{1,0:T(8,128)S(1)}, f32[2,256,256]{2,1,0:T(8,128)S(1)}, f32[256,256]{1,0:T(8,128)S(1)}, f32[256,256]{1,0:T(8,128)S(1)}) custom-call(f32[2048,256]{1,0:T(8,128)S(1)} %slice_select_fusion.1.xr_in, f32[256,1024]{1,0:T(8,128)S(1)} %broadcast_select_fusion.1.xct_in, ...), custom_call_target="tpu_custom_call" | custom-call | tf_op jit(solution)/shard_map/spread_panel_0/pallas_call | solution.py:287
  55.2 2.2 convolution_add_fusion.1
  57.4 4.4 %convolution_select_fusion.1.part = f32[256,1024]{1,0:T(8,128)S(1)} fusion(f32[2048,256]{0,1:T(8,128)S(1)} %convolution_add_fusion.1, f32[2048,1024]{1,0:T(8,128)S(1)} %bitcast.79, pred[1024]{0:T(1024)(128)(4,1)S(1)} %get-tuple-element.106), kind=kOutput, calls=%fused_computation.41 | convolution fusion | flops 3221487616 | bytes 11535360 | tf_op jit(solution)/shard_map/dot_general | solution.py:493
  61.9 1.1 convolution_add_fusion.3.vec_cols
  63.0 82.2 %reduce_product_0.1 = (f32[256,1024]{1,0:T(8,128)S(1)}, f32[2,256,1024]{2,1,0:T(8,128)S(1)}, f32[256,256]{1,0:T(8,128)S(1)}, f32[4,8,8,256]{3,2,1,0:T(8,128)S(1)}) custom-call(f32[256,1024]{1,0:T(8,128)S(1)} %convolution_select_fusion.1.part, f32[256,256]{1,0:T(8,128)S(1)} %slice_bitcast_fusion.1.top, f32[256,256]{1,0:T(8,128)S(1)} %get-tuple-element.72.lower_inverse, ...), custom_call_target="tpu_custom_call" | custom-call | tf_op jit(solution)/shard_map/reduce_product_0/pallas_call | solution.py:446
  145.2 0.0 copy-start
  145.2 1.0 copy-done
  146.2 0.7 copy-done.8
  146.9 2.2 reshape.229
  149.1 1.9 copy.4
  151.0 0.0 copy-start.13
  151.0 0.0 copy-start.9
  151.0 0.0 slice-start.6
  151.0 2.0 fusion.53
  153.1 0.0 copy-done.9
  153.1 0.4 fusion.54
  153.5 0.4 fusion.55
  153.9 0.0 copy-done.13
  153.9 0.0 slice-start.7
  153.9 2.1 fusion.15
  156.0 1.0 fusion.56
  157.1 1.0 fusion.25
  158.2 9.1 %fusion.11 = f32[2048,1024]{1,0:T(8,128)} fusion(f32[2048,1024]{1,0:T(8,128)S(1)} %bitcast.82, f32[2048,256]{0,1:T(8,128)S(1)} %copy-done.13, f32[2048,256]{0,1:T(8,128)S(1)} %fusion.15, f32[256,1024]{1,0:T(8,128)S(1)} %fusion.25, f32[256,1024]{1,0:T(8,128)S(1)} %convolution_add_fusion.3.vec_cols), kind=kOutput, calls=%fused_computation.9 | convolution fusion | flops 6446120960 | bytes 23068672 | tf_op jit(solution)/shard_map/dot_general | solution.py:18
  167.3 0.7 compare_reduce_fusion
  168.1 3.6 %fusion.16 = f32[2048,1024]{1,0:T(8,128)} fusion(f32[2048,1024]{1,0:T(8,128)} %fusion.11, pred[2048]{0:T(1024)(128)(4,1)S(1)} %get-tuple-element.100, pred[]{:T(512)S(6)} %eq.74, pred[]{:T(512)} %compare_reduce_fusion, f32[256,256]{1,0:T(8,128)S(1)} %get-tuple-element.94, pred[2048]{0:T(1024)(128)(4,1)S(1)} %get-tuple-element.96), kind=kLoop, calls=%fused_computation.18 | loop fusion | flops 2097152 | bytes 4461057 | tf_op jit(solution)/shard_map/scatter | solution.py:510
  171.6 0.1 copy.5
  171.8 0.2 tile.18
  172.0 0.2 copy.10
  172.2 2.5 broadcast_select_fusion
  174.7 1.9 slice_select_fusion.xr_in
  176.7 3.5 %fusion.57.gram_in = f32[256,256]{1,0:T(8,128)S(1)} fusion(f32[2048,256]{1,0:T(8,128)S(1)} %slice_select_fusion.xr_in), kind=kOutput, calls=%fused_computation.102 | convolution fusion | flops 1610612736 | bytes 2359296 | tf_op jit(solution)/shard_map/dot_general | solution.py:22
  180.1 0.0 slice-start.1
  180.2 42.5 %spread_panel_1.1 = (f32[2048,256]{1,0:T(8,128)S(1)}, f32[256,1024]{1,0:T(8,128)S(1)}, f32[2,256,256]{2,1,0:T(8,128)S(1)}, f32[256,256]{1,0:T(8,128)S(1)}, f32[256,256]{1,0:T(8,128)S(1)}) custom-call(f32[2048,256]{1,0:T(8,128)S(1)} %slice_select_fusion.xr_in, f32[256,1024]{1,0:T(8,128)S(1)} %get-tuple-element.89.xct_in, f32[256,256]{1,0:T(8,128)S(1)} %fusion.57.gram_in, ...), custom_call_target="tpu_custom_call" | custom-call | tf_op jit(solution)/shard_map/spread_panel_1/pallas_call | solution.py:287
  222.7 2.1 convolution_add_fusion
  224.8 4.2 %convolution_select_fusion.part = f32[256,1024]{1,0:T(8,128)S(1)} fusion(f32[2048,256]{0,1:T(8,128)S(1)} %convolution_add_fusion, f32[2048,1024]{1,0:T(8,128)S(1)} %bitcast.73, pred[1024]{0:T(1024)(128)(4,1)S(1)} %get-tuple-element.105), kind=kOutput, calls=%fused_computation.40 | convolution fusion | flops 3221487616 | bytes 11535360 | tf_op jit(solution)/shard_map/dot_general | solution.py:493
  229.1 1.1 convolution_add_fusion.2.vec_cols
  230.2 71.7 %reduce_product_1.1 = (f32[256,1024]{1,0:T(8,128)S(1)}, f32[2,256,1024]{2,1,0:T(8,128)S(1)}, f32[256,256]{1,0:T(8,128)S(1)}, f32[4,8,8,256]{3,2,1,0:T(8,128)S(1)}) custom-call(f32[256,1024]{1,0:T(8,128)S(1)} %convolution_select_fusion.part, f32[256,256]{1,0:T(8,128)S(1)} %slice_bitcast_fusion.top, f32[256,256]{1,0:T(8,128)S(1)} %get-tuple-element.81.lower_inverse, ...), custom_call_target="tpu_custom_call" | custom-call | tf_op jit(solution)/shard_map/reduce_product_1/pallas_call | solution.py:446
  301.9 1.0 copy-done.2
  302.9 0.7 copy-done.10
  303.6 2.2 reshape.232
  305.8 1.9 copy.6
  307.8 0.0 slice-start.2
  307.8 2.0 fusion.58
  309.8 0.4 fusion.59
  310.2 0.4 fusion.60
  310.7 0.0 slice-start.3
  310.7 2.1 fusion.14
  312.8 1.0 fusion.61
  313.8 1.0 fusion.24
  314.9 9.1 %fusion.8 = f32[2048,1024]{1,0:T(8,128)} fusion(f32[2048,1024]{1,0:T(8,128)S(1)} %bitcast.75, f32[2048,256]{0,1:T(8,128)S(1)} %copy-done.15, f32[2048,256]{0,1:T(8,128)S(1)} %fusion.14, f32[256,1024]{1,0:T(8,128)S(1)} %fusion.24, f32[256,1024]{1,0:T(8,128)S(1)} %convolution_add_fusion.2.vec_cols), kind=kOutput, calls=%fused_computation.8 | convolution fusion | flops 6446120960 | bytes 23068672 | tf_op jit(solution)/shard_map/dot_general | solution.py:18
  324.1 3.7 %fusion.17 = f32[2048,1024]{1,0:T(8,128)} fusion(f32[2048,1024]{1,0:T(8,128)} %fusion.8, pred[2048]{0:T(1024)(128)(4,1)S(1)} %get-tuple-element.99, pred[]{:T(512)S(6)} %eq.82, pred[]{:T(512)} %compare_reduce_fusion, f32[256,256]{1,0:T(8,128)S(1)} %get-tuple-element.92, pred[2048]{0:T(1024)(128)(4,1)S(1)} %get-tuple-element.95), kind=kLoop, calls=%fused_computation.19 | loop fusion | flops 2097152 | bytes 4461057 | tf_op jit(solution)/shard_map/scatter | solution.py:510
  327.8 0.1 copy.7
  328.0 0.2 tile.42
  328.2 0.2 copy.11
  328.4 2.4 fusion.26
  330.8 10.5 %reshape.235 = f32[8,256,4,256]{3,2,1,0:T(4,128)} reshape(f32[2048,1024]{1,0:T(8,128)} %fusion.26) | data formatting | bytes 16777216 | tf_op jit(solution)/shard_map/reshape | solution.py:518
  (48 shorter events, 0.3 us)
Async XLA Ops:
  12.3 45.1 %slice-start.4 = ((s8[8388608]{0:T(1024)(128)(4,1)}), s8[4194304]{0:T(1024)(128)(4,1)S(1)}, s32[]{:S(2)}) async-start(s8[8388608]{0:T(1024)(128)(4,1)} %bitcast.77), calls=%async_computation.4 | async-start | bytes 8388608
  15.9 41.4 %slice-start.5 = ((s8[8388608]{0:T(1024)(128)(4,1)}), s8[4194304]{0:T(1024)(128)(4,1)S(1)}, s32[]{:S(2)}) async-start(s8[8388608]{0:T(1024)(128)(4,1)} %bitcast.77), calls=%async_computation.5 | async-start | bytes 8388608
  55.2 2.2 copy-start.4
  57.4 4.5 %copy-start.12 = (f32[2048,256]{0,1:T(8,128)}, f32[2048,256]{0,1:T(8,128)S(1)}, u32[]{:S(2)}) copy-start(f32[2048,256]{0,1:T(8,128)S(1)} %convolution_add_fusion.1) | copy-start | bytes 6291460
  145.2 1.0 copy-start
  146.2 0.7 copy-start.8
  151.0 2.9 copy-start.13
  151.0 2.0 copy-start.9
  151.0 7.1 %slice-start.6 = ((s8[8388608]{0:T(1024)(128)(4,1)}), s8[4194304]{0:T(1024)(128)(4,1)S(1)}, s32[]{:S(2)}) async-start(s8[8388608]{0:T(1024)(128)(4,1)} %bitcast.80), calls=%async_computation.6 | async-start | bytes 8388608
  153.9 2.1 copy-start.1
  153.9 4.2 %slice-start.7 = ((s8[8388608]{0:T(1024)(128)(4,1)}), s8[4194304]{0:T(1024)(128)(4,1)S(1)}, s32[]{:S(2)}) async-start(s8[8388608]{0:T(1024)(128)(4,1)} %bitcast.80), calls=%async_computation.7 | async-start | bytes 8388608
  158.1 9.9 %copy-start.5 = (f32[256,256]{1,0:T(8,128)S(1)}, f32[256,256]{1,0:T(8,128)}, u32[]{:S(2)}) copy-start(f32[256,256]{1,0:T(8,128)} %copy-done.4) | copy-start | bytes 786436
  174.7 50.1 %slice-start = ((s8[8388608]{0:T(1024)(128)(4,1)}), s8[4194304]{0:T(1024)(128)(4,1)S(1)}, s32[]{:S(2)}) async-start(s8[8388608]{0:T(1024)(128)(4,1)} %bitcast.72), calls=%async_computation | async-start | bytes 8388608
  180.1 44.7 %slice-start.1 = ((s8[8388608]{0:T(1024)(128)(4,1)}), s8[4194304]{0:T(1024)(128)(4,1)S(1)}, s32[]{:S(2)}) async-start(s8[8388608]{0:T(1024)(128)(4,1)} %bitcast.72), calls=%async_computation.1 | async-start | bytes 8388608
  222.6 2.2 copy-start.6
  224.8 4.2 %copy-start.14 = (f32[2048,256]{0,1:T(8,128)}, f32[2048,256]{0,1:T(8,128)S(1)}, u32[]{:S(2)}) copy-start(f32[2048,256]{0,1:T(8,128)S(1)} %convolution_add_fusion) | copy-start | bytes 6291460
  301.9 1.0 copy-start.2
  302.9 0.7 copy-start.10
  307.8 2.9 copy-start.15
  307.8 2.0 copy-start.11
  307.8 7.1 %slice-start.2 = ((s8[8388608]{0:T(1024)(128)(4,1)}), s8[4194304]{0:T(1024)(128)(4,1)S(1)}, s32[]{:S(2)}) async-start(s8[8388608]{0:T(1024)(128)(4,1)} %bitcast.74), calls=%async_computation.2 | async-start | bytes 8388608
  310.7 2.1 copy-start.3
  310.7 4.2 %slice-start.3 = ((s8[8388608]{0:T(1024)(128)(4,1)}), s8[4194304]{0:T(1024)(128)(4,1)S(1)}, s32[]{:S(2)}) async-start(s8[8388608]{0:T(1024)(128)(4,1)} %bitcast.74), calls=%async_computation.3 | async-start | bytes 8388608
  314.9 9.2 %copy-start.7 = (f32[256,256]{1,0:T(8,128)S(1)}, f32[256,256]{1,0:T(8,128)}, u32[]{:S(2)}) copy-start(f32[256,256]{1,0:T(8,128)} %copy-done.6) | copy-start | bytes 786436
